TPU v7x, 32 devices: a whole 2x2x4 slice. The times are simulated.
32 devices in a mesh: dp: 8 (over z, y), tensor: 4 (over x, core).
Axes of the slice: x: 2, y: 2, z: 4, core: 2. Of those that a mesh axis runs over, the one named last changes fastest.
Arguments:
- hidden: bfloat16 [2, 512, 8192], P(None, 'dp', 'tensor'), may hold values from -6 to 6
- query_weight: bfloat16 [8192, 4096], P('tensor'), may hold values from -0.0625 to 0.0625
- key_weight: bfloat16 [8192, 512], P('tensor'), may hold values from -0.0625 to 0.0625
- value_weight: bfloat16 [8192, 512], P('tensor'), may hold values from -0.0625 to 0.0625
- adapter_down_weight: bfloat16 [8, 8192, 192], P('dp', 'tensor'), may hold values from -0.0625 to 0.0625
- adapter_up_query: bfloat16 [8, 64, 4096], P('dp', None, 'tensor'), may hold values from -0.75 to 0.75
- adapter_up_key_value: bfloat16 [8, 2, 64, 512], P('dp', None, None, 'tensor'), may hold values from -0.75 to 0.75
- cached_keys: bfloat16 [512, 96, 512], P('dp', None, 'tensor'), may hold values from -136 to 136
- cached_values: bfloat16 [512, 96, 512], P('dp', None, 'tensor'), may hold values from -6 to 6
- adapter_index: int32 [512, 1], P('dp'), may hold values from 0 to 7; in each aligned block of 64 rows (0 to 63, 64 to 127, ...) at most 16 rows name the same one
- cache_length: int32 [512], P('dp'), may hold values from 1 to 96, as said below
Outputs:
- attended: bfloat16 [2, 512, 4096], P(None, 'dp', 'tensor')
Inputs may be any that keep to these rules, and one draw needn't show every extreme that they name: `adapter_index`: among the 64 requests of one device (aligned blocks of rows) no adapter is named more than 16 times, a bound that some block reaches. `cache_length`: one request of every device has a full cache of 96 positions.
All inputs are finite; a program needn't handle non-finite values.
Results may differ from a plain program's by a relative error of at most 0.012.
The roundings to bfloat16 on the way count: a program that leaves them out, or rounds other values in their place, can miss the bound.
Values may be sent and summed in bfloat16 or wider, within the bound.
A program may use at most 128 MiB of HBM per device.

v0:
```python
import jax
import jax.numpy as jnp
from jax import lax
from jax.sharding import PartitionSpec as P

HEAD_WIDTH = 128


adapter_scale = 0.5


def shards(
    hidden,
    query_weight,
    key_weight,
    value_weight,
    adapter_down_weight,
    adapter_up_query,
    adapter_up_key_value,
    cached_keys,
    cached_values,
    adapter_index,
    cache_length,
):
    step_count, request_count, part_width = hidden.shape
    row_count = step_count * request_count
    flat_rows = hidden.reshape(row_count, part_width)
    part_query = jnp.dot(flat_rows, query_weight, preferred_element_type=jnp.float32)
    part_key = jnp.dot(flat_rows, key_weight, preferred_element_type=jnp.float32)
    part_value = jnp.dot(flat_rows, value_weight, preferred_element_type=jnp.float32)
    plain_query, plain_key, plain_value = (
        lax.psum_scatter(part_query, "tensor", scatter_dimension=1, tiled=True),
        lax.psum_scatter(part_key, "tensor", scatter_dimension=1, tiled=True),
        lax.psum_scatter(part_value, "tensor", scatter_dimension=1, tiled=True),
    )
    query_width = plain_query.shape[1]
    kv_width = plain_key.shape[1]
    rank_span = adapter_up_query.shape[1]
    chosen = adapter_index[:, 0]
    owners = lax.axis_size("dp")
    capacity = max(2, 2 * request_count // owners)
    slot_rows = capacity * step_count
    onehot = (chosen[:, None] == jnp.arange(owners, dtype=jnp.int32)[None, :]).astype(jnp.int32)
    order = jnp.sum(onehot * (jnp.cumsum(onehot, axis=0) - 1), axis=1)
    target = chosen * capacity + order
    dispatch = (jnp.arange(owners * capacity, dtype=jnp.int32)[:, None] == target[None, :]).astype(
        jnp.bfloat16
    )
    outgoing = jnp.einsum(
        "mr,srd->msd", dispatch, hidden, preferred_element_type=jnp.float32
    ).astype(jnp.bfloat16)
    outgoing = outgoing.reshape(owners, slot_rows, part_width)
    terms = jnp.einsum(
        "nsd,ndk->nsk",
        outgoing,
        lax.all_gather(adapter_down_weight, "dp", axis=0, tiled=True),
        preferred_element_type=jnp.float32,
    )
    shrunk = lax.psum(terms, "tensor").astype(jnp.bfloat16)
    start_sums = (
        jnp.zeros((owners, slot_rows, query_width), jnp.float32),
        jnp.zeros((owners, slot_rows, kv_width), jnp.float32),
        jnp.zeros((owners, slot_rows, kv_width), jnp.float32),
    )
    query_up_weight = lax.all_gather(adapter_up_query, "dp", axis=0, tiled=True)
    key_value_up_weight = lax.all_gather(adapter_up_key_value, "dp", axis=0, tiled=True)
    term_query = jnp.einsum(
        "nsr,nrq->nsq", shrunk[..., :rank_span], query_up_weight, preferred_element_type=jnp.float32
    )
    term_key = jnp.einsum(
        "nsr,nrq->nsq",
        shrunk[..., rank_span : 2 * rank_span],
        key_value_up_weight[:, 0],
        preferred_element_type=jnp.float32,
    )
    term_value = jnp.einsum(
        "nsr,nrq->nsq",
        shrunk[..., 2 * rank_span :],
        key_value_up_weight[:, 1],
        preferred_element_type=jnp.float32,
    )
    results = []
    for total, term in (
        (start_sums[0], term_query),
        (start_sums[1], term_key),
        (start_sums[2], term_value),
    ):
        results.append(term)
    sum_query = results[0]
    sum_key = results[1]
    sum_value = results[2]
    returned = jnp.concatenate(
        [
            sum_query.astype(jnp.bfloat16),
            sum_key.astype(jnp.bfloat16),
            sum_value.astype(jnp.bfloat16),
        ],
        axis=2,
    )
    returned = returned.reshape(owners * capacity, step_count, query_width + 2 * kv_width)
    combined = jnp.einsum(
        "mr,msw->srw", dispatch, returned, preferred_element_type=jnp.float32
    ).astype(jnp.bfloat16)
    combined = combined.reshape(row_count, query_width + 2 * kv_width)
    query_update = combined[:, :query_width]
    key_update = combined[:, query_width : query_width + kv_width]
    value_update = combined[:, query_width + kv_width :]
    query_rows = (plain_query + adapter_scale * query_update.astype(jnp.float32)).astype(
        jnp.bfloat16
    )
    appended_keys = (plain_key + adapter_scale * key_update.astype(jnp.float32)).astype(
        jnp.bfloat16
    )
    appended_values = (plain_value + adapter_scale * value_update.astype(jnp.float32)).astype(
        jnp.bfloat16
    )
    local_heads = query_width // HEAD_WIDTH
    local_kv = kv_width // HEAD_WIDTH
    group_width = local_heads // local_kv
    cache_depth = cached_keys.shape[1]
    head_rows = query_rows.reshape(step_count, request_count, local_kv, group_width, HEAD_WIDTH)
    fresh_keys = appended_keys.reshape(step_count, request_count, local_kv, HEAD_WIDTH)
    fresh_values = appended_values.reshape(step_count, request_count, local_kv, HEAD_WIDTH)
    prior_keys = cached_keys.reshape(request_count, cache_depth, local_kv, HEAD_WIDTH)
    prior_values = cached_values.reshape(request_count, cache_depth, local_kv, HEAD_WIDTH)
    factor = HEAD_WIDTH ** (-0.5)
    scores_old = (
        jnp.einsum("srkgd,rckd->srkgc", head_rows, prior_keys, preferred_element_type=jnp.float32)
        * factor
    )
    scores_new = (
        jnp.einsum("srkgd,trkd->srkgt", head_rows, fresh_keys, preferred_element_type=jnp.float32)
        * factor
    )
    valid_old = jnp.arange(cache_depth, dtype=jnp.int32)[None, :] < cache_length[:, None]
    valid_new = (
        jnp.arange(step_count, dtype=jnp.int32)[None, :]
        <= jnp.arange(step_count, dtype=jnp.int32)[:, None]
    )
    scores_old = jnp.where(valid_old[None, :, None, None, :], scores_old, -1e30)
    scores_new = jnp.where(valid_new[:, None, None, None, :], scores_new, -1e30)
    highest = jnp.maximum(jnp.max(scores_old, axis=-1), jnp.max(scores_new, axis=-1))
    exp_old = jnp.exp(scores_old - highest[..., None])
    exp_new = jnp.exp(scores_new - highest[..., None])
    denominator = jnp.sum(exp_old, axis=-1) + jnp.sum(exp_new, axis=-1)
    weight_old = (exp_old / denominator[..., None]).astype(jnp.bfloat16)
    weight_new = (exp_new / denominator[..., None]).astype(jnp.bfloat16)
    mixed = jnp.einsum(
        "srkgc,rckd->srkgd", weight_old, prior_values, preferred_element_type=jnp.float32
    )
    mixed = mixed + jnp.einsum(
        "srkgt,trkd->srkgd", weight_new, fresh_values, preferred_element_type=jnp.float32
    )
    return mixed.reshape(step_count, request_count, query_width).astype(jnp.bfloat16)


def solution(mesh):
    return jax.shard_map(
        shards,
        mesh=mesh,
        in_specs=(
            P(None, "dp", "tensor"),
            P("tensor", None),
            P("tensor", None),
            P("tensor", None),
            P("dp", "tensor", None),
            P("dp", None, "tensor"),
            P("dp", None, None, "tensor"),
            P("dp", None, "tensor"),
            P("dp", None, "tensor"),
            P("dp", None),
            P("dp"),
        ),
        out_specs=P(None, "dp", "tensor"),
        check_vma=False,
    )
```

profile of v0, /device:TPU:0, one launch (start us, length us, event | category | flops | bytes accessed | tf_op | source)
XLA Modules:
  0.0 173.8 jit_solution(6041073350771258585)
XLA Ops:
  7.4 0.0 copy-start
  7.4 0.0 all-gather.3.cloned.1.call-start
  7.4 0.7 all-gather.3.cloned.1.call-update
  8.1 0.0 all-gather.5.cloned.1.call-start
  8.1 0.7 all-gather.5.cloned.1.call-update
  8.8 0.0 reduce-scatter.4.cloned.1.call-start
  8.9 9.6 %fusion.54 = f32[128,4096]{1,0:T(8,128)} fusion(bf16[128,2048]{1,0:T(8,128)(2,1)} %bitcast.115, bf16[2048,4096]{1,0:T(8,128)(2,1)} %param.12), kind=kOutput, calls=%fused_computation.58 | convolution fusion | flops 2147483648 | bytes 19398656 | tf_op jit(solution)/shard_map/dot_general | solution.py:28
  18.5 0.0 copy-start.1
  18.5 0.0 reduce-scatter.4.cloned.1.call-update
  18.6 0.0 reduce-scatter.6.cloned.1.call-start
  18.6 0.0 copy-done
  18.6 1.0 copy-done.1
  19.6 1.2 fusion.56
  20.7 0.0 copy-start.3
  20.7 0.0 reduce-scatter.6.cloned.1.call-update
  20.8 0.0 reduce-scatter.8.cloned.1.call-start
  20.8 2.9 %fusion.57 = f32[128,512]{1,0:T(8,128)} fusion(bf16[128,2048]{1,0:T(8,128)(2,1)S(1)} %bitcast.117, bf16[2048,512]{1,0:T(8,128)(2,1)} %param.14), kind=kOutput, calls=%fused_computation.61 | convolution fusion | flops 268435456 | bytes 2883584 | tf_op jit(solution)/shard_map/dot_general | solution.py:30
  23.8 0.0 reduce-scatter.8.cloned.1.call-update
  23.8 0.0 copy-done.3
  23.8 0.1 fusion.46
  23.9 0.1 reduce_window_sum.11
  24.0 0.2 select_reduce_fusion
  24.2 0.6 convolution_convert_fusion
  24.7 0.0 copy-start.2
  24.8 0.0 copy-start.4
  24.8 1.1 copy.27
  25.8 1.2 reshape.129
  27.1 0.0 copy-done.2
  27.1 33.5 %all_gather.11 = bf16[8,2,64,128]{3,2,0,1:T(8,128)(2,1)S(1)} all-gather(bf16[1,2,64,128]{3,2,0,1:T(8,128)(2,1)S(1)} %bitcast.122), channel_id=1, replica_groups=mesh['dp'=8,'tensor'=4] {'dp'}, dimensions={0}, use_global_device_ids=true | all-gather | bytes 294912 | tf_op jit(solution)/shard_map/all_gather | solution.py:66
  60.6 0.0 copy-done.4
  60.6 0.1 iota_compare_fusion.2
  60.6 53.8 %all-gather.3.cloned.1.call-done = bf16[8,2048,192]{1,2,0:T(8,128)(2,1)} async-done(((bf16[1,2048,192]{1,2,0:T(8,128)(2,1)}), bf16[8,2048,192]{1,2,0:T(8,128)(2,1)}) %all-gather.3.cloned.1.call-update) | async-done | bytes 6291472 | tf_op jit(solution)/shard_map/all_gather | solution.py:56
  114.5 5.2 %fusion.55 = f32[8,32,192]{2,1,0:T(8,128)S(1)} fusion(bf16[8,32,2048]{2,1,0:T(8,128)(2,1)} %reshape.129, bf16[8,2048,192]{1,2,0:T(8,128)(2,1)} %all-gather.3.cloned.1.call-done), kind=kOutput, calls=%fused_computation.59 | convolution fusion | flops 201326592 | bytes 7536640 | tf_op jit(solution)/shard_map/nsd,ndk->nsk/dot_general | solution.py:53
  119.6 14.3 %all-reduce.1 = bf16[8,32,192]{2,1,0:T(8,128)(2,1)S(1)} all-reduce(f32[8,32,192]{2,1,0:T(8,128)S(1)} %fusion.55), channel_id=1, replica_groups=mesh['dp'=8,'tensor'=4] {'tensor'}, use_global_device_ids=true, to_apply=%region_3.0 | all-reduce | flops 49152 | bytes 294912 | tf_op jit(solution)/shard_map/psum | solution.py:59
  133.9 0.2 convolution_convert_fusion.3
  134.1 0.2 convolution_convert_fusion.4
  134.3 21.0 %all-gather.5.cloned.1.call-done = bf16[8,64,1024]{2,1,0:T(8,128)(2,1)} async-done(((bf16[1,64,1024]{2,1,0:T(8,128)(2,1)}), bf16[8,64,1024]{2,1,0:T(8,128)(2,1)}) %all-gather.5.cloned.1.call-update) | async-done | bytes 1048592 | tf_op jit(solution)/shard_map/all_gather | solution.py:65
  155.3 1.5 convolution_convert_fusion.2
  156.9 0.1 pad_maximum_fusion
  156.9 0.2 reshape.130
  157.2 0.3 convolution_convert_fusion.1
  157.5 0.0 reduce-scatter.4.cloned.1.call-done
  157.5 1.1 fusion.32
  158.7 0.0 reduce-scatter.6.cloned.1.call-done
  158.7 0.0 reduce-scatter.8.cloned.1.call-done
  158.8 0.9 add_convert_fusion.1
  159.6 1.3 fusion.53
  160.9 2.5 %fusion.52 = (f32[2,64,8]{2,0,1:T(2,128)S(1)}, f32[2,64,1,8,96]{4,3,0,1,2:T(8,128)S(1)}) fusion(bf16[64,96,128]{2,1,0:T(8,128)(2,1)} %param.18, pred[64,96]{1,0:T(8,128)(4,1)S(1)} %iota_compare_fusion.2, bf16[2,64,8,128]{3,2,1,0:T(8,128)(2,1)S(1)} %bitcast.121), kind=kOutput, calls=%fused_computation.56 | convolution fusion | flops 25459712 | bytes 2238464 | tf_op jit(solution)/shard_map/srkgd,rckd->srkgc/dot_general | solution.py:128
  163.4 0.0 copy-start.5
  163.4 0.3 fusion.37
  163.7 0.4 fusion.31
  164.2 0.3 fusion.41
  164.5 0.3 copy-done.5
  164.8 0.6 fusion.25
  165.4 0.1 convert_element_type.80
  165.5 0.8 copy.34
  (5 shorter events, 0.1 us)
Async XLA Ops:
  7.4 11.3 %copy-start = (bf16[2048,512]{1,0:T(8,128)(2,1)S(1)}, bf16[2048,512]{1,0:T(8,128)(2,1)}, u32[]{:S(2)}) copy-start(bf16[2048,512]{1,0:T(8,128)(2,1)} %param.13) | copy-start | bytes 6291460
  7.4 107.1 %all-gather.3.cloned.1.call-start = ((), (), s32[]{:S(2)}) async-start(), calls=%async_computation.4 | async-start | bytes 7077888 | tf_op jit(solution)/shard_map/all_gather | solution.py:56
  8.1 147.3 %all-gather.5.cloned.1.call-start = ((), (), s32[]{:S(2)}) async-start(), calls=%async_computation.5 | async-start | bytes 1179648 | tf_op jit(solution)/shard_map/all_gather | solution.py:65
  8.8 148.7 %reduce-scatter.4.cloned.1.call-start = ((), (), s32[]{:S(2)}) async-start(), calls=%async_computation.3 | async-start | bytes 2621440 | tf_op jit(solution)/shard_map/reduce_scatter | solution.py:32
  18.5 1.0 copy-start.1
  18.6 140.2 %reduce-scatter.6.cloned.1.call-start = ((), (), s32[]{:S(2)}) async-start(), calls=%async_computation.6 | async-start | bytes 327680 | tf_op jit(solution)/shard_map/reduce_scatter | solution.py:33
  20.7 3.1 %copy-start.3 = (s32[64,1]{0,1:T(1,128)S(1)}, s32[64,1]{0,1:T(1,128)}, u32[]{:S(2)}) copy-start(s32[64,1]{0,1:T(1,128)} %param.20) | copy-start | bytes 772
  20.8 138.0 %reduce-scatter.8.cloned.1.call-start = ((), (), s32[]{:S(2)}) async-start(), calls=%async_computation.7 | async-start | bytes 327680 | tf_op jit(solution)/shard_map/reduce_scatter | solution.py:34
  24.7 2.3 %copy-start.2 = (bf16[1,2,64,128]{3,2,1,0:T(8,128)(2,1)S(1)}, bf16[1,2,64,128]{3,2,1,0:T(8,128)(2,1)}, u32[]{:S(2)}) copy-start(bf16[1,2,64,128]{3,2,1,0:T(8,128)(2,1)} %param.17) | copy-start | bytes 98308
  24.8 35.8 %copy-start.4 = (s32[64]{0:T(128)S(1)}, s32[64]{0:T(128)}, u32[]{:S(2)}) copy-start(s32[64]{0:T(128)} %param.21) | copy-start | bytes 772
  163.4 1.4 copy-start.5
Sparse Core Ops, SparseCore 0:
  10.6 103.8 all-gather.2
  116.8 38.4 all-gather.4
Sparse Core Ops, SparseCore 1:
  18.6 34.1 reduce-scatter.3
  55.3 20.0 reduce-scatter.5
  77.6 19.9 reduce-scatter.7
where the time goes:
time: 174 us
  waiting for transfers between devices  76.4 us (44%)
  blocking collectives  47.8 us (27%)
  matrix products  26.3 us (15%)
  between operations  15.2 us (9%)
  local copies, waits for them, and re-layouts  4.66 us (3%)
  other arithmetic  3.27 us (2%)
    all_gather x1, waiting for transfers between devices, shards(): lax.all_gather(adapter_down_weight, 'dp', axis=0, tiled=True)  53.8 us
    all_gather x1, blocking collectives, shards(): lax.all_gather(adapter_up_key_value, 'dp', axis=0, tiled=True)  33.5 us
    all_gather x1, waiting for transfers between devices, shards(): query_up_weight = lax.all_gather(adapter_up_query, 'dp', axis=0, tiled=True)  21 us
    psum x1, blocking collectives, shards(): shrunk = lax.psum(terms, 'tensor').astype(jnp.bfloat16)  14.3 us
    dot_general x1, matrix products, shards(): jnp.dot(flat_rows, query_weight, preferred_element_type=jnp.float32)  9.65 us
    dot_general x1, matrix products, shards(): jnp.einsum('nsd,ndk->nsk', outgoing, lax.all_gather(adapter_down_weight,...  5.17 us
  transfers between devices with their start and end apart: 5, of which 2 were waited for; matrix products, arithmetic and copies ran while one was open for 15% of the time, Pallas kernels for 0%

commit v1 on v0

--- a/solution.py
+++ b/solution.py
@@ -50,53 +50,31 @@
         "mr,srd->msd", dispatch, hidden, preferred_element_type=jnp.float32
     ).astype(jnp.bfloat16)
     outgoing = outgoing.reshape(owners, slot_rows, part_width)
-    terms = jnp.einsum(
-        "nsd,ndk->nsk",
-        outgoing,
-        lax.all_gather(adapter_down_weight, "dp", axis=0, tiled=True),
+    arrived = lax.all_to_all(outgoing, "dp", 0, 0).reshape(owners * slot_rows, part_width)
+    terms = jnp.dot(arrived, adapter_down_weight[0], preferred_element_type=jnp.float32)
+    shrunk = lax.psum(terms, "tensor").astype(jnp.bfloat16)
+    sum_query = jnp.dot(
+        shrunk[:, :rank_span], adapter_up_query[0], preferred_element_type=jnp.float32
+    )
+    sum_key = jnp.dot(
+        shrunk[:, rank_span : 2 * rank_span],
+        adapter_up_key_value[0, 0],
         preferred_element_type=jnp.float32,
     )
-    shrunk = lax.psum(terms, "tensor").astype(jnp.bfloat16)
-    start_sums = (
-        jnp.zeros((owners, slot_rows, query_width), jnp.float32),
-        jnp.zeros((owners, slot_rows, kv_width), jnp.float32),
-        jnp.zeros((owners, slot_rows, kv_width), jnp.float32),
-    )
-    query_up_weight = lax.all_gather(adapter_up_query, "dp", axis=0, tiled=True)
-    key_value_up_weight = lax.all_gather(adapter_up_key_value, "dp", axis=0, tiled=True)
-    term_query = jnp.einsum(
-        "nsr,nrq->nsq", shrunk[..., :rank_span], query_up_weight, preferred_element_type=jnp.float32
-    )
-    term_key = jnp.einsum(
-        "nsr,nrq->nsq",
-        shrunk[..., rank_span : 2 * rank_span],
-        key_value_up_weight[:, 0],
+    sum_value = jnp.dot(
+        shrunk[:, 2 * rank_span :],
+        adapter_up_key_value[0, 1],
         preferred_element_type=jnp.float32,
     )
-    term_value = jnp.einsum(
-        "nsr,nrq->nsq",
-        shrunk[..., 2 * rank_span :],
-        key_value_up_weight[:, 1],
-        preferred_element_type=jnp.float32,
-    )
-    results = []
-    for total, term in (
-        (start_sums[0], term_query),
-        (start_sums[1], term_key),
-        (start_sums[2], term_value),
-    ):
-        results.append(term)
-    sum_query = results[0]
-    sum_key = results[1]
-    sum_value = results[2]
     returned = jnp.concatenate(
         [
             sum_query.astype(jnp.bfloat16),
             sum_key.astype(jnp.bfloat16),
             sum_value.astype(jnp.bfloat16),
         ],
-        axis=2,
+        axis=1,
     )
+    returned = lax.all_to_all(returned.reshape(owners, slot_rows, -1), "dp", 0, 0)
     returned = returned.reshape(owners * capacity, step_count, query_width + 2 * kv_width)
     combined = jnp.einsum(
         "mr,msw->srw", dispatch, returned, preferred_element_type=jnp.float32

time: 174 us -> 105 us (0.60)
  waiting for transfers between devices: 76.4 us -> 32.5 us
  blocking collectives: 47.8 us -> 12.1 us
  starting transfers between devices: 0.17 us -> 13.6 us
  matrix products: 26.3 us -> 21 us
  local copies, waits for them, and re-layouts: 4.66 us -> 7.35 us
  between operations: 15.2 us -> 13.3 us
    all_gather x2 -> x0, waiting for transfers between devices: 74.9 us -> none  [the longest x1 53.8 us: shards(): lax.all_gather(adapter_down_weight, 'dp', axis=0, tiled=True)]
    all_gather x1 -> x0, blocking collectives: 33.5 us -> none  [shards(): lax.all_gather(adapter_up_key_value, 'dp', axis=0, tiled=True)]
    all_to_all x0 -> x2, waiting for transfers between devices: none -> 29.8 us  [the longest x1 16.3 us: shards(): lax.all_to_all(returned.reshape(owners, slot_rows, -1), 'dp', 0, 0)]
    all_to_all x0 -> x2, starting transfers between devices: none -> 13.5 us  [the longest x1 7.29 us: shards(): lax.all_to_all(outgoing, 'dp', 0, 0).reshape(owners * slot_rows, part_width)]
    dot_general x4, matrix products: 7.05 us -> 2.42 us  [the longest x1 1.73 us: shards(): jnp.dot(arrived, adapter_down_weight[0], preferred_element_type=jnp.float32)]
    reduce_scatter x1, waiting for transfers between devices: 0.03 us -> 2.61 us  [shards(): lax.psum_scatter(part_query, 'tensor', scatter_dimension=1, tiled=True)]
    psum x1, blocking collectives: 14.3 us -> 12.1 us  [shards(): shrunk = lax.psum(terms, 'tensor').astype(jnp.bfloat16)]
  transfers between devices with their start and end apart: 5 -> 5, of which waited for: 2 -> 3; matrix products, arithmetic and copies ran while one was open for 15% -> 21% of each run, Pallas kernels for 0% -> 0%
where the time goes in v1:
time: 105 us; the launch traced here: 104 us
  waiting for transfers between devices  32.5 us (31%)
  matrix products  21 us (20%)
  starting transfers between devices  13.6 us (13%)
  between operations  13.3 us (13%)
  blocking collectives  12.1 us (12%)
  local copies, waits for them, and re-layouts  7.35 us (7%)
  other arithmetic  4.22 us (4%)
    all_to_all x1, waiting for transfers between devices, shards(): lax.all_to_all(returned.reshape(owners, slot_rows, -1), 'dp', 0, 0)  16.3 us
    all_to_all x1, waiting for transfers between devices, shards(): lax.all_to_all(outgoing, 'dp', 0, 0).reshape(owners * slot_rows, part_width)  13.5 us
    psum x1, blocking collectives, shards(): shrunk = lax.psum(terms, 'tensor').astype(jnp.bfloat16)  12.1 us
    dot_general x1, matrix products, shards(): jnp.dot(flat_rows, query_weight, preferred_element_type=jnp.float32)  9.52 us
    all_to_all x1, starting transfers between devices, shards(): lax.all_to_all(outgoing, 'dp', 0, 0).reshape(owners * slot_rows, part_width)  7.29 us
    all_to_all x1, starting transfers between devices, shards(): lax.all_to_all(returned.reshape(owners, slot_rows, -1), 'dp', 0, 0)  6.23 us
    dot_general x1, matrix products, shards(): jnp.dot(flat_rows, value_weight, preferred_element_type=jnp.float32)  2.75 us
    reduce_scatter x1, waiting for transfers between devices, shards(): lax.psum_scatter(part_query, 'tensor', scatter_dimension=1, tiled=True)  2.61 us
  transfers between devices with their start and end apart: 5, of which 3 were waited for; matrix products, arithmetic and copies ran while one was open for 21% of the time, Pallas kernels for 0%

profile of v1, /device:TPU:0, one launch (start us, length us, event | category | flops | bytes accessed | tf_op | source)
XLA Modules:
  0.0 104.1 jit_solution(3879688252768387095)
XLA Ops:
  6.5 0.0 copy-start
  6.5 0.0 copy-start.1
  6.5 0.0 copy-start.6
  6.5 0.0 reduce-scatter.6.cloned.1.call-start
  6.5 1.6 %copy-done = bf16[2048,512]{1,0:T(8,128)(2,1)S(1)} copy-done((bf16[2048,512]{1,0:T(8,128)(2,1)S(1)}, bf16[2048,512]{1,0:T(8,128)(2,1)}, u32[]{:S(2)}) %copy-start) | copy-done | bytes 2097176
  8.1 2.2 %fusion.62 = f32[128,512]{1,0:T(8,128)} fusion(bf16[128,2048]{1,0:T(8,128)(2,1)} %bitcast.120, bf16[2048,512]{1,0:T(8,128)(2,1)S(1)} %copy-done), kind=kOutput, calls=%fused_computation.64 | convolution fusion | flops 268435456 | bytes 2883584 | tf_op jit(solution)/shard_map/dot_general | solution.py:29
  10.3 0.0 reduce-scatter.6.cloned.1.call-update
  10.4 0.0 copy-done.6
  10.4 0.1 fusion.49
  10.4 0.1 reduce_window_sum.11
  10.5 0.2 select_reduce_fusion
  10.7 0.0 copy-done.1
  10.7 0.5 convolution_convert_fusion
  11.3 2.1 %copy.19 = bf16[128,2,2048]{2,1,0:T(2,128)(2,1)} copy(bf16[128,2,2048]{2,0,1:T(8,128)(2,1)S(1)} %convolution_convert_fusion) | data formatting | bytes 2097152 | tf_op jit(solution)/shard_map/convert_element_type | solution.py:51
  13.4 2.3 %reshape.135 = bf16[8,32,2048]{2,1,0:T(8,128)(2,1)} reshape(bf16[128,2,2048]{2,1,0:T(2,128)(2,1)} %copy.19) | data formatting | bytes 2097152 | tf_op jit(solution)/shard_map/reshape | solution.py:52
  15.6 7.3 %all-to-all-start = ((bf16[8,32,2048]{2,1,0:T(8,128)(2,1)}), bf16[8,32,2048]{2,1,0:T(8,128)(2,1)}, u32[]{:S(2)}, u32[]{:S(2)}) async-start(bf16[8,32,2048]{2,1,0:T(8,128)(2,1)} %reshape.135), calls=%async_computation.1 | async-start | bytes 2097152 | tf_op jit(solution)/shard_map/all_to_all | solution.py:53
  22.9 0.0 reduce-scatter.8.cloned.1.call-start
  23.0 2.7 %fusion.63 = f32[128,512]{1,0:T(8,128)} fusion(bf16[128,2048]{1,0:T(8,128)(2,1)S(1)} %bitcast.121, bf16[2048,512]{1,0:T(8,128)(2,1)} %param.14), kind=kOutput, calls=%fused_computation.65 | convolution fusion | flops 268435456 | bytes 2883584 | tf_op jit(solution)/shard_map/dot_general | solution.py:30
  25.7 0.0 reduce-scatter.8.cloned.1.call-update
  25.7 0.0 reduce-scatter.4.cloned.1.call-start
  25.8 9.5 %fusion.61 = f32[128,4096]{1,0:T(8,128)} fusion(bf16[128,2048]{1,0:T(8,128)(2,1)S(1)} %bitcast.122, bf16[2048,4096]{1,0:T(8,128)(2,1)} %param.12), kind=kOutput, calls=%fused_computation.63 | convolution fusion | flops 2147483648 | bytes 19398656 | tf_op jit(solution)/shard_map/dot_general | solution.py:28
  35.3 0.0 copy-start.3
  35.3 0.0 copy-start.5
  35.3 0.0 copy-start.4
  35.3 0.0 reduce-scatter.4.cloned.1.call-update
  35.3 13.5 %all-to-all-done = bf16[8,32,2048]{2,1,0:T(8,128)(2,1)} async-done(((bf16[8,32,2048]{2,1,0:T(8,128)(2,1)}), bf16[8,32,2048]{2,1,0:T(8,128)(2,1)}, u32[]{:S(2)}, u32[]{:S(2)}) %all-to-all-start) | async-done | bytes 1048608 | tf_op jit(solution)/shard_map/all_to_all | solution.py:53
  48.8 0.0 copy-done.3
  48.8 1.7 %fusion.30 = f32[256,192]{0,1:T(8,128)S(1)} fusion(bf16[256,2048]{1,0:T(8,128)(2,1)} %bitcast.3, bf16[1,2048,192]{1,2,0:T(8,128)(2,1)S(1)} %copy-done.3), kind=kOutput, calls=%fused_computation.20 | convolution fusion | flops 201326592 | bytes 2031616 | tf_op jit(solution)/shard_map/dot_general | solution.py:54
  50.5 0.0 copy-start.7
  50.5 12.1 %all-reduce.1 = bf16[256,192]{0,1:T(8,128)(2,1)S(1)} all-reduce(f32[256,192]{0,1:T(8,128)S(1)} %fusion.30), channel_id=1, replica_groups=mesh['dp'=8,'tensor'=4] {'tensor'}, use_global_device_ids=true, to_apply=%region_3.0 | all-reduce | flops 49152 | bytes 294912 | tf_op jit(solution)/shard_map/psum | solution.py:55
  62.7 0.0 copy-done.5
  62.7 0.2 convolution_convert_fusion.3
  62.9 0.2 convolution_convert_fusion.4
  63.1 0.0 copy-done.4
  63.1 0.3 convolution_convert_fusion.2
  63.4 0.9 pad_maximum_fusion
  64.3 6.2 %all-to-all-start.1 = ((bf16[8,32,1280]{2,1,0:T(8,128)(2,1)}), bf16[8,32,1280]{2,1,0:T(8,128)(2,1)S(1)}, u32[]{:S(2)}, u32[]{:S(2)}) async-start(bf16[8,32,1280]{2,1,0:T(8,128)(2,1)} %bitcast.8), calls=%async_computation.2 | async-start | bytes 1310720 | tf_op jit(solution)/shard_map/all_to_all | solution.py:77
  70.5 0.0 copy-done.7
  70.5 0.1 iota_compare_fusion.2
  70.6 16.3 %all-to-all-done.1 = bf16[8,32,1280]{2,1,0:T(8,128)(2,1)S(1)} async-done(((bf16[8,32,1280]{2,1,0:T(8,128)(2,1)}), bf16[8,32,1280]{2,1,0:T(8,128)(2,1)S(1)}, u32[]{:S(2)}, u32[]{:S(2)}) %all-to-all-start.1) | async-done | bytes 655392 | tf_op jit(solution)/shard_map/all_to_all | solution.py:77
  86.9 0.2 reshape.138
  87.2 0.3 convolution_convert_fusion.1
  87.5 0.0 reduce-scatter.6.cloned.1.call-done
  87.5 0.0 reduce-scatter.8.cloned.1.call-done
  87.5 0.9 add_convert_fusion.1
  88.4 2.6 %reduce-scatter.4.cloned.1.call-done = f32[128,1024]{1,0:T(8,128)} async-done(((f32[128,4096]{1,0:T(8,128)}), f32[128,1024]{1,0:T(8,128)}) %reduce-scatter.4.cloned.1.call-update) | async-done | bytes 524304 | tf_op jit(solution)/shard_map/reduce_scatter | solution.py:32
  91.1 0.0 copy-start.2
  91.1 1.2 %fusion.34 = bf16[16,8,8,128]{3,1,2,0:T(8,128)(2,1)S(1)} fusion(f32[128,1024]{1,0:T(8,128)} %reduce-scatter.4.cloned.1.call-done, bf16[128,1280]{1,0:T(8,128)(2,1)S(1)} %bitcast.124), kind=kLoop, calls=%fused_computation.28 | loop fusion | flops 524288 | bytes 1048576
  92.3 1.3 %fusion.60 = (f32[2,64,8]{2,0,1:T(2,128)S(1)}, f32[2,64,1,8,2]{3,4,0,1,2:T(2,128)S(1)}) fusion(bf16[2,64,128,1]{2,1,0,3:T(8,128)(2,1)S(1)} %bitcast.128, pred[2,2]{1,0:T(4,128)(4,1)S(1)} %iota_compare_fusion.3, bf16[2,64,8,128]{3,2,1,0:T(8,128)(2,1)S(1)} %bitcast.125), kind=kOutput, calls=%fused_computation.62 | convolution fusion | flops 529408 | bytes 307204 | tf_op jit(solution)/shard_map/srkgd,trkd->srkgt/dot_general | solution.py:110
  93.6 0.0 copy-done.2
  93.6 1.0 fusion.59
  94.7 0.0 copy-start.8
  94.7 0.3 fusion.40
  95.0 0.4 fusion.33
  95.5 0.3 fusion.41
  95.8 0.3 copy-done.8
  96.1 0.6 fusion.25
  96.7 0.1 convert_element_type.80
  96.8 0.8 copy.27
  (5 shorter events, 0.1 us)
Async XLA Ops:
  6.5 1.6 %copy-start = (bf16[2048,512]{1,0:T(8,128)(2,1)S(1)}, bf16[2048,512]{1,0:T(8,128)(2,1)}, u32[]{:S(2)}) copy-start(bf16[2048,512]{1,0:T(8,128)(2,1)} %param.13) | copy-start | bytes 6291460
  6.5 4.2 %copy-start.1 = (bf16[2,64,2048]{2,1,0:T(8,128)(2,1)S(1)}, bf16[2,64,2048]{2,1,0:T(8,128)(2,1)}, u32[]{:S(2)}) copy-start(bf16[2,64,2048]{2,1,0:T(8,128)(2,1)} %param.11) | copy-start | bytes 1572868
  6.5 3.8 %copy-start.6 = (s32[64,1]{0,1:T(1,128)S(1)}, s32[64,1]{0,1:T(1,128)}, u32[]{:S(2)}) copy-start(s32[64,1]{0,1:T(1,128)} %param.20) | copy-start | bytes 772
  6.5 81.0 %reduce-scatter.6.cloned.1.call-start = ((), (), s32[]{:S(2)}) async-start(), calls=%async_computation.6 | async-start | bytes 327680 | tf_op jit(solution)/shard_map/reduce_scatter | solution.py:33
  15.6 33.2 %all-to-all-start = ((bf16[8,32,2048]{2,1,0:T(8,128)(2,1)}), bf16[8,32,2048]{2,1,0:T(8,128)(2,1)}, u32[]{:S(2)}, u32[]{:S(2)}) async-start(bf16[8,32,2048]{2,1,0:T(8,128)(2,1)} %reshape.135), calls=%async_computation.1 | async-start | bytes 2097152 | tf_op jit(solution)/shard_map/all_to_all | solution.py:53
  22.9 64.6 %reduce-scatter.8.cloned.1.call-start = ((), (), s32[]{:S(2)}) async-start(), calls=%async_computation.7 | async-start | bytes 327680 | tf_op jit(solution)/shard_map/reduce_scatter | solution.py:34
  25.7 65.3 %reduce-scatter.4.cloned.1.call-start = ((), (), s32[]{:S(2)}) async-start(), calls=%async_computation.5 | async-start | bytes 2621440 | tf_op jit(solution)/shard_map/reduce_scatter | solution.py:32
  35.3 13.5 %copy-start.3 = (bf16[1,2048,192]{1,2,0:T(8,128)(2,1)S(1)}, bf16[1,2048,192]{1,2,0:T(8,128)(2,1)}, u32[]{:S(2)}) copy-start(bf16[1,2048,192]{1,2,0:T(8,128)(2,1)} %param.15) | copy-start | bytes 2359300
  35.3 27.4 %copy-start.5 = (bf16[1,2,64,128]{3,2,1,0:T(8,128)(2,1)S(1)}, bf16[1,2,64,128]{3,2,1,0:T(8,128)(2,1)}, u32[]{:S(2)}) copy-start(bf16[1,2,64,128]{3,2,1,0:T(8,128)(2,1)} %param.17) | copy-start | bytes 98308
  35.3 27.8 %copy-start.4 = (bf16[1,64,1024]{2,1,0:T(8,128)(2,1)S(1)}, bf16[1,64,1024]{2,1,0:T(8,128)(2,1)}, u32[]{:S(2)}) copy-start(bf16[1,64,1024]{2,1,0:T(8,128)(2,1)} %param.16) | copy-start | bytes 393220
  50.5 20.0 %copy-start.7 = (s32[64]{0:T(128)S(1)}, s32[64]{0:T(128)}, u32[]{:S(2)}) copy-start(s32[64]{0:T(128)} %param.21) | copy-start | bytes 772
  64.3 22.7 %all-to-all-start.1 = ((bf16[8,32,1280]{2,1,0:T(8,128)(2,1)}), bf16[8,32,1280]{2,1,0:T(8,128)(2,1)S(1)}, u32[]{:S(2)}, u32[]{:S(2)}) async-start(bf16[8,32,1280]{2,1,0:T(8,128)(2,1)} %bitcast.8), calls=%async_computation.2 | async-start | bytes 1310720 | tf_op jit(solution)/shard_map/all_to_all | solution.py:77
  91.1 2.6 %copy-start.2 = (bf16[64,96,128]{2,1,0:T(8,128)(2,1)S(1)}, bf16[64,96,128]{2,1,0:T(8,128)(2,1)}, u32[]{:S(2)}) copy-start(bf16[64,96,128]{2,1,0:T(8,128)(2,1)} %param.18) | copy-start | bytes 4718596
  94.7 1.4 %copy-start.8 = (bf16[64,96,128]{2,1,0:T(8,128)(2,1)S(1)}, bf16[64,96,128]{2,1,0:T(8,128)(2,1)}, u32[]{:S(2)}) copy-start(bf16[64,96,128]{2,1,0:T(8,128)(2,1)} %param.19) | copy-start | bytes 4718596
Sparse Core Ops, SparseCore 0:
  10.5 22.7 reduce-scatter.5
  35.9 20.0 reduce-scatter.7
  58.5 32.4 reduce-scatter.3

commit v2 on v1

v2 whole, which is shorter than its diff:
```python
import functools

import jax
import jax.numpy as jnp
from jax import lax
from jax.experimental import pallas as pl
from jax.experimental.pallas import tpu as pltpu
from jax.sharding import PartitionSpec as P

HEAD_WIDTH = 128
MESH = pl.DeviceIdType.MESH

adapter_scale = 0.5


def project_kernel(
    owners,
    hid_ref, disp_ref, back_ref, down_ref, up_ref, wq_ref, wk_ref, wv_ref,
    out_ref,
    wbuf, part, rs1, rs2, outgoing, arrived, terms, terms_in, sums, sums_in, delta, returned,
    w_sem, d_send, d_recv, r_send, r_recv, x_send, x_recv,
):
    me = lax.axis_index("dp")
    t = lax.axis_index("tensor")
    pair = t + 1 - 2 * (t % 2)
    across = (t + 2) % 4
    targets = {0: t, 1: pair, 2: across, 3: (pair + 2) % 4}
    order = (3, 2, 1, 0)
    width = part.shape[2]
    q_width = wq_ref.shape[1] // 4
    kv_width = wk_ref.shape[1] // 4

    def weight_copies(k):
        q_cols = pl.ds(pl.multiple_of(targets[k] * q_width, 128), q_width)
        kv_cols = pl.ds(pl.multiple_of(targets[k] * kv_width, 128), kv_width)
        return (
            pltpu.make_async_copy(
                wq_ref.at[:, q_cols], wbuf.at[k, :, pl.ds(0, q_width)], w_sem.at[k, 0]
            ),
            pltpu.make_async_copy(
                wk_ref.at[:, kv_cols], wbuf.at[k, :, pl.ds(q_width, kv_width)], w_sem.at[k, 1]
            ),
            pltpu.make_async_copy(
                wv_ref.at[:, kv_cols],
                wbuf.at[k, :, pl.ds(q_width + kv_width, kv_width)],
                w_sem.at[k, 2],
            ),
        )

    for k in order:
        for copy in weight_copies(k):
            copy.start()

    barrier = pltpu.get_barrier_semaphore()

    @pl.loop(1, owners)
    def _(i):
        pl.semaphore_signal(
            barrier, inc=1, device_id={"dp": (me + i) % owners}, device_id_type=MESH
        )

    for peer in (pair, across):
        pl.semaphore_signal(barrier, inc=1, device_id={"tensor": peer}, device_id_type=MESH)
    pl.semaphore_wait(barrier, owners + 1)

    def dispatch_copy(i):
        return pltpu.make_async_remote_copy(
            src_ref=outgoing.at[i],
            dst_ref=arrived.at[i],
            send_sem=d_send.at[i],
            recv_sem=d_recv.at[i],
            device_id={"dp": (me + i) % owners},
            device_id_type=MESH,
        )

    def return_copy(i):
        return pltpu.make_async_remote_copy(
            src_ref=delta.at[i],
            dst_ref=returned.at[i],
            send_sem=r_send.at[i],
            recv_sem=r_recv.at[i],
            device_id={"dp": (me + owners - i) % owners},
            device_id_type=MESH,
        )

    def tensor_copy(src, dst, number, peer):
        return pltpu.make_async_remote_copy(
            src_ref=src,
            dst_ref=dst,
            send_sem=x_send.at[number],
            recv_sem=x_recv.at[number],
            device_id={"tensor": peer},
            device_id_type=MESH,
        )

    def picked(i):
        return jnp.dot(
            disp_ref[i], hid_ref[...], preferred_element_type=jnp.float32
        ).astype(jnp.bfloat16)

    @pl.loop(1, owners)
    def _(i):
        outgoing[i] = picked(i)
        dispatch_copy(i).start()

    arrived[0] = picked(0)

    tile = 256

    def project(k):
        for copy in weight_copies(k):
            copy.wait()

        @pl.loop(0, width // tile)
        def _(c):
            cols = pl.ds(pl.multiple_of(c * tile, tile), tile)
            part[k, :, cols] = jnp.dot(
                hid_ref[...], wbuf[k, :, cols], preferred_element_type=jnp.float32
            )

    own_copy = tensor_copy(part.at[1], rs1.at[0], 0, pair)
    far_copy = tensor_copy(part.at[3], rs1.at[1], 1, pair)
    sum_copy = tensor_copy(part.at[2], rs2, 2, across)
    project(3)
    far_copy.start()
    project(2)
    far_copy.wait()
    part[2] = part[2] + rs1[1]
    sum_copy.start()
    project(1)
    own_copy.start()
    project(0)

    def shrink(i):
        terms[i] = jnp.dot(arrived[i], down_ref[...], preferred_element_type=jnp.float32)

    shrink(0)

    @pl.loop(1, owners)
    def _(i):
        dispatch_copy(i).wait()
        shrink(i)

    terms_copy = tensor_copy(terms, terms_in, 3, pair)
    terms_copy.start()
    terms_copy.wait()
    sums[...] = terms[...] + terms_in[...]
    sums_copy = tensor_copy(sums, sums_in, 4, across)
    sums_copy.start()
    sums_copy.wait()

    def expand(i):
        shrunk = (sums[i] + sums_in[i]).astype(jnp.bfloat16)
        return jnp.dot(
            shrunk, up_ref[...], preferred_element_type=jnp.float32
        ).astype(jnp.bfloat16)

    @pl.loop(1, owners)
    def _(i):
        delta[i] = expand(i)
        return_copy(i).start()

    returned[0] = expand(0)
    own_copy.wait()
    sum_copy.wait()
    part[0] = part[0] + rs1[0] + rs2[...]

    def combine(i):
        part[1] = part[1] + jnp.dot(
            back_ref[i], returned[i], preferred_element_type=jnp.float32
        )

    part[1] = jnp.zeros(part.shape[1:], jnp.float32)
    combine(0)

    @pl.loop(1, owners)
    def _(i):
        return_copy(i).wait()
        combine(i)

    out_ref[...] = (part[0] + adapter_scale * part[1]).astype(jnp.bfloat16)


def shards(
    hidden,
    query_weight,
    key_weight,
    value_weight,
    adapter_down_weight,
    adapter_up_query,
    adapter_up_key_value,
    cached_keys,
    cached_values,
    adapter_index,
    cache_length,
):
    step_count, request_count, part_width = hidden.shape
    row_count = step_count * request_count
    flat_rows = hidden.reshape(row_count, part_width)
    owners = lax.axis_size("dp")
    rank_span = adapter_up_query.shape[1]
    query_width = adapter_up_query.shape[2]
    kv_width = adapter_up_key_value.shape[3]
    width = query_width + 2 * kv_width
    rank_pad = -(-3 * rank_span // 128) * 128
    capacity = max(2, 2 * request_count // owners)
    slot_rows = capacity * step_count
    chosen = adapter_index[:, 0]
    places = jnp.arange(request_count, dtype=jnp.int32)
    earlier = (chosen[:, None] == chosen[None, :]) & (places[None, :] < places[:, None])
    order = jnp.sum(earlier.astype(jnp.int32), axis=1)
    offset = (chosen - lax.axis_index("dp") + owners) % owners
    steps = jnp.arange(step_count, dtype=jnp.int32)
    slot = (offset * slot_rows + order)[None, :] + capacity * steps[:, None]
    slot = slot.reshape(row_count)
    numbers = jnp.arange(owners * slot_rows, dtype=jnp.int32)
    dispatch = (numbers.reshape(owners, slot_rows, 1) == slot[None, None, :]).astype(jnp.bfloat16)
    back = (numbers.reshape(owners, 1, slot_rows) == slot[None, :, None]).astype(jnp.bfloat16)
    down = jnp.pad(adapter_down_weight[0], ((0, 0), (0, rank_pad - 3 * rank_span)))
    up = jnp.concatenate(
        [
            jnp.pad(adapter_up_query[0], ((0, rank_pad - rank_span), (0, 0))),
            jnp.pad(adapter_up_key_value[0, 0], ((rank_span, rank_pad - 2 * rank_span), (0, 0))),
            jnp.pad(
                adapter_up_key_value[0, 1], ((2 * rank_span, rank_pad - 3 * rank_span), (0, 0))
            ),
        ],
        axis=1,
    )
    f32, bf16 = jnp.float32, jnp.bfloat16
    vmem = pl.BlockSpec(memory_space=pltpu.VMEM)
    hbm = pl.BlockSpec(memory_space=pl.ANY)
    rows = pl.pallas_call(
        functools.partial(project_kernel, owners),
        out_shape=jax.ShapeDtypeStruct((row_count, width), bf16),
        in_specs=[vmem] * 5 + [hbm] * 3,
        out_specs=vmem,
        scratch_shapes=[
            pltpu.VMEM((4, part_width, width), bf16),
            pltpu.VMEM((4, row_count, width), f32),
            pltpu.VMEM((2, row_count, width), f32),
            pltpu.VMEM((row_count, width), f32),
            pltpu.VMEM((owners, slot_rows, part_width), bf16),
            pltpu.VMEM((owners, slot_rows, part_width), bf16),
            pltpu.VMEM((owners, slot_rows, rank_pad), f32),
            pltpu.VMEM((owners, slot_rows, rank_pad), f32),
            pltpu.VMEM((owners, slot_rows, rank_pad), f32),
            pltpu.VMEM((owners, slot_rows, rank_pad), f32),
            pltpu.VMEM((owners, slot_rows, width), bf16),
            pltpu.VMEM((owners, slot_rows, width), bf16),
            pltpu.SemaphoreType.DMA((4, 3)),
            pltpu.SemaphoreType.DMA((owners,)),
            pltpu.SemaphoreType.DMA((owners,)),
            pltpu.SemaphoreType.DMA((owners,)),
            pltpu.SemaphoreType.DMA((owners,)),
            pltpu.SemaphoreType.DMA((5,)),
            pltpu.SemaphoreType.DMA((5,)),
        ],
        compiler_params=pltpu.CompilerParams(
            collective_id=0, has_side_effects=True, vmem_limit_bytes=52 * 1024 * 1024
        ),
    )(flat_rows, dispatch, back, down, up, query_weight, key_weight, value_weight)
    query_rows = rows[:, :query_width]
    appended_keys = rows[:, query_width : query_width + kv_width]
    appended_values = rows[:, query_width + kv_width :]
    local_heads = query_width // HEAD_WIDTH
    local_kv = kv_width // HEAD_WIDTH
    group_width = local_heads // local_kv
    cache_depth = cached_keys.shape[1]
    head_rows = query_rows.reshape(step_count, request_count, local_kv, group_width, HEAD_WIDTH)
    fresh_keys = appended_keys.reshape(step_count, request_count, local_kv, HEAD_WIDTH)
    fresh_values = appended_values.reshape(step_count, request_count, local_kv, HEAD_WIDTH)
    prior_keys = cached_keys.reshape(request_count, cache_depth, local_kv, HEAD_WIDTH)
    prior_values = cached_values.reshape(request_count, cache_depth, local_kv, HEAD_WIDTH)
    factor = HEAD_WIDTH ** (-0.5)
    scores_old = (
        jnp.einsum("srkgd,rckd->srkgc", head_rows, prior_keys, preferred_element_type=jnp.float32)
        * factor
    )
    scores_new = (
        jnp.einsum("srkgd,trkd->srkgt", head_rows, fresh_keys, preferred_element_type=jnp.float32)
        * factor
    )
    valid_old = jnp.arange(cache_depth, dtype=jnp.int32)[None, :] < cache_length[:, None]
    valid_new = (
        jnp.arange(step_count, dtype=jnp.int32)[None, :]
        <= jnp.arange(step_count, dtype=jnp.int32)[:, None]
    )
    scores_old = jnp.where(valid_old[None, :, None, None, :], scores_old, -1e30)
    scores_new = jnp.where(valid_new[:, None, None, None, :], scores_new, -1e30)
    highest = jnp.maximum(jnp.max(scores_old, axis=-1), jnp.max(scores_new, axis=-1))
    exp_old = jnp.exp(scores_old - highest[..., None])
    exp_new = jnp.exp(scores_new - highest[..., None])
    denominator = jnp.sum(exp_old, axis=-1) + jnp.sum(exp_new, axis=-1)
    weight_old = (exp_old / denominator[..., None]).astype(jnp.bfloat16)
    weight_new = (exp_new / denominator[..., None]).astype(jnp.bfloat16)
    mixed = jnp.einsum(
        "srkgc,rckd->srkgd", weight_old, prior_values, preferred_element_type=jnp.float32
    )
    mixed = mixed + jnp.einsum(
        "srkgt,trkd->srkgd", weight_new, fresh_values, preferred_element_type=jnp.float32
    )
    return mixed.reshape(step_count, request_count, query_width).astype(jnp.bfloat16)


def solution(mesh):
    return jax.shard_map(
        shards,
        mesh=mesh,
        in_specs=(
            P(None, "dp", "tensor"),
            P("tensor", None),
            P("tensor", None),
            P("tensor", None),
            P("dp", "tensor", None),
            P("dp", None, "tensor"),
            P("dp", None, None, "tensor"),
            P("dp", None, "tensor"),
            P("dp", None, "tensor"),
            P("dp", None),
            P("dp"),
        ),
        out_specs=P(None, "dp", "tensor"),
        check_vma=False,
    )
```

time: 105 us -> 67.3 us (0.64)
  Pallas kernels: 0 us -> 57.2 us
  waiting for transfers between devices: 32.5 us -> 0 us
  matrix products: 21 us -> 3.28 us
  starting transfers between devices: 13.6 us -> 0 us
  between operations: 13.3 us -> 0.18 us
  blocking collectives: 12.1 us -> 0 us
  local copies, waits for them, and re-layouts: 7.35 us -> 3.65 us
  other arithmetic: 4.22 us -> 2.84 us
    pallas_call x0 -> x1, Pallas kernels: none -> 57.2 us  [shards(): pl.pallas_call(functools.partial(project_kernel, owners), out_shape=jax.S...]
    all_to_all x2 -> x0, waiting for transfers between devices: 29.8 us -> none  [the longest x1 16.3 us: shards(): lax.all_to_all(returned.reshape(owners, slot_rows, -1), 'dp', 0, 0)]
    dot_general x9 -> x0, matrix products: 17.7 us -> none  [the longest x1 9.52 us: shards(): jnp.dot(flat_rows, query_weight, preferred_element_type=jnp.float32)]
    all_to_all x2 -> x0, starting transfers between devices: 13.5 us -> none  [the longest x1 7.29 us: shards(): lax.all_to_all(outgoing, 'dp', 0, 0).reshape(owners * slot_rows, part_width)]
    psum x1 -> x0, blocking collectives: 12.1 us -> none  [shards(): shrunk = lax.psum(terms, 'tensor').astype(jnp.bfloat16)]
    reduce_scatter x3 -> x0, waiting for transfers between devices: 2.65 us -> none  [the longest x1 2.61 us: shards(): lax.psum_scatter(part_query, 'tensor', scatter_dimension=1, tiled=True)]
    reshape x2 -> x0, local copies, waits for them, and re-layouts: 2.51 us -> none  [the longest x1 2.26 us: shards(): outgoing = outgoing.reshape(owners, slot_rows, part_width)]
    convert_element_type x1 -> x0, local copies, waits for them, and re-layouts: 2.07 us -> none  [shards(): outgoing = jnp.einsum('mr,srd->msd', dispatch, hidden, preferred_element_...]
  transfers between devices with their start and end apart: 5 -> 0, of which waited for: 3 -> 0; matrix products, arithmetic and copies ran while one was open for 21% -> 0% of each run, Pallas kernels for 0% -> 0%
where the time goes in v2:
time: 67.3 us; the launch traced here: 67.1 us
  Pallas kernels  57.2 us (85%)
  local copies, waits for them, and re-layouts  3.65 us (5%)
  matrix products  3.28 us (5%)
  other arithmetic  2.84 us (4%)
    pallas_call x1, Pallas kernels, shards(): pl.pallas_call(functools.partial(project_kernel, owners), out_shape=jax.S...  57.2 us
    unnamed x15, local copies, waits for them, and re-layouts  1.57 us

profile of v2, /device:TPU:0, one launch (start us, length us, event | category | flops | bytes accessed | tf_op | source)
XLA Modules:
  0.0 67.1 jit_solution(16131715406211478406)
XLA Ops:
  0.0 0.0 copy-start
  0.0 1.0 %convert_reduce_fusion = s32[64]{0:T(128)S(1)} fusion(s32[64]{0:T(128)} %bitcast.104), kind=kLoop, calls=%fused_computation.43 | loop fusion | flops 20416 | bytes 512 | tf_op jit(solution)/shard_map/reduce_sum | solution.py:211
  1.0 0.7 %fusion.49 = s32[64]{0:T(128)S(1)} fusion(s32[64]{0:T(128)S(1)} %convert_reduce_fusion, s32[]{:T(128)S(6)} %axis_index.15, s32[64,1]{0,1:T(1,128)} %param.20), kind=kLoop, calls=%fused_computation.55 | loop fusion | flops 960 | bytes 772 | tf_op jit(solution)/shard_map/add | solution.py:214
  1.7 0.1 broadcast_add_fusion
  1.7 0.1 add.95
  1.8 0.1 compare_convert_fusion.1.disp_ref
  1.9 0.1 compare_convert_fusion.back_ref
  2.1 0.0 copy-start.4
  2.1 0.0 copy-start.3
  2.1 1.5 %copy.18 = bf16[1,2048,192]{2,1,0:T(8,128)(2,1)S(1)} copy(bf16[1,2048,192]{1,2,0:T(8,128)(2,1)} %param.15) | data formatting | bytes 1572864 | tf_op args[4]
  3.6 0.0 copy-start.1
  3.6 1.2 %pad.16.down_ref = bf16[2048,256]{1,0:T(8,128)(2,1)} pad(bf16[2048,192]{1,0:T(8,128)(2,1)S(1)} %bitcast.98, bf16[]{:T(256)} %constant.37.clone.1), padding=0_0x0_64 | pad | bytes 1835010 | tf_op jit(solution)/shard_map/jit(_pad)/pad | solution.py:219
  4.7 0.0 copy-done.4
  4.7 0.0 copy-done.3
  4.8 0.0 copy-done.1
  4.8 57.2 %shard_map.109 = bf16[128,1280]{1,0:T(8,128)(2,1)S(1)} custom-call(bf16[128,2048]{1,0:T(8,128)(2,1)S(1)} %bitcast.97, bf16[8,32,128]{2,1,0:T(8,128)(2,1)S(1)} %compare_convert_fusion.1.disp_ref, bf16[8,128,32]{2,1,0:T(8,128)(2,1)S(1)} %compare_convert_fusion.back_ref, bf16[2048,256]{1,0:T(8,128)(2,1)} %pad.16.down_ref, bf16[256,1280]{1,0:T(8,128)(2,1)S(1)} %fusion.35.up_ref, ...), custom_call_target="tpu_custom_call" | custom-call | tf_op jit(solution)/shard_map/pallas_call | solution.py:233
  62.0 0.0 copy-start.5
  62.0 0.0 copy-start.2
  62.1 1.3 %fusion.53 = (f32[2,64,8]{2,0,1:T(2,128)S(1)}, f32[2,64,1,8,2]{3,4,0,1,2:T(2,128)S(1)}) fusion(bf16[2,64,128,1]{2,1,0,3:T(8,128)(2,1)S(1)} %bitcast.103, pred[2,2]{1,0:T(4,128)(4,1)S(1)} %iota_compare_fusion.6, bf16[2,64,8,128]{3,2,1,0:T(8,128)(2,1)S(1)} %bitcast.99), kind=kOutput, calls=%fused_computation.61 | convolution fusion | flops 529408 | bytes 307204 | tf_op jit(solution)/shard_map/srkgd,trkd->srkgt/dot_general | solution.py:281
  63.4 0.0 copy-done.5
  63.4 0.1 iota_compare_fusion.5
  63.5 0.0 copy-done.2
  63.5 1.0 %fusion.52 = (f32[2,64,8]{2,0,1:T(2,128)S(1)}, f32[2,64,1,8,96]{4,3,0,1,2:T(8,128)S(1)}) fusion(bf16[64,96,128]{2,1,0:T(8,128)(2,1)S(1)} %copy-done.2, pred[64,96]{1,0:T(8,128)(4,1)S(1)} %iota_compare_fusion.5, bf16[2,64,8,128]{3,2,1,0:T(8,128)(2,1)S(1)} %bitcast.100), kind=kOutput, calls=%fused_computation.60 | convolution fusion | flops 25459712 | bytes 2238464 | tf_op jit(solution)/shard_map/srkgd,rckd->srkgc/dot_general | solution.py:277
  64.6 0.4 fusion.36
  65.0 0.3 fusion.41
  65.3 0.3 fusion.42
  65.7 0.0 copy-done
  65.7 0.6 fusion.29
  66.3 0.1 convert_element_type.43
  66.4 0.8 %copy.23 = bf16[2,64,1024]{2,1,0:T(8,128)(2,1)} copy(bf16[2,64,1024]{2,0,1:T(2,128)(2,1)S(1)} %convert_element_type.43) | data formatting | bytes 524288 | tf_op jit(solution)/shard_map/convert_element_type | solution.py:303
  (10 shorter events, 0.2 us)
Async XLA Ops:
  0.0 65.7 %copy-start = (bf16[64,96,128]{2,1,0:T(8,128)(2,1)S(1)}, bf16[64,96,128]{2,1,0:T(8,128)(2,1)}, u32[]{:S(2)}) copy-start(bf16[64,96,128]{2,1,0:T(8,128)(2,1)} %param.19) | copy-start | bytes 4718596
  2.1 2.7 %copy-start.4 = (bf16[1,2,64,128]{3,2,1,0:T(8,128)(2,1)S(1)}, bf16[1,2,64,128]{3,2,1,0:T(8,128)(2,1)}, u32[]{:S(2)}) copy-start(bf16[1,2,64,128]{3,2,1,0:T(8,128)(2,1)} %param.17) | copy-start | bytes 98308
  2.1 2.7 %copy-start.3 = (bf16[1,64,1024]{2,1,0:T(8,128)(2,1)S(1)}, bf16[1,64,1024]{2,1,0:T(8,128)(2,1)}, u32[]{:S(2)}) copy-start(bf16[1,64,1024]{2,1,0:T(8,128)(2,1)} %param.16) | copy-start | bytes 393220
  3.6 1.2 %copy-start.1 = (bf16[2,64,2048]{2,1,0:T(8,128)(2,1)S(1)}, bf16[2,64,2048]{2,1,0:T(8,128)(2,1)}, u32[]{:S(2)}) copy-start(bf16[2,64,2048]{2,1,0:T(8,128)(2,1)} %param.11) | copy-start | bytes 1572868
  62.0 1.4 %copy-start.5 = (s32[64]{0:T(128)S(1)}, s32[64]{0:T(128)}, u32[]{:S(2)}) copy-start(s32[64]{0:T(128)} %param.21) | copy-start | bytes 772
  62.0 1.5 %copy-start.2 = (bf16[64,96,128]{2,1,0:T(8,128)(2,1)S(1)}, bf16[64,96,128]{2,1,0:T(8,128)(2,1)}, u32[]{:S(2)}) copy-start(bf16[64,96,128]{2,1,0:T(8,128)(2,1)} %param.18) | copy-start | bytes 4718596

commit v3 on v2

--- a/solution.py
+++ b/solution.py
@@ -27,6 +27,17 @@
     targets = {0: t, 1: pair, 2: across, 3: (pair + 2) % 4}
     order = (3, 2, 1, 0)
     width = part.shape[2]
+    rank = down_ref.shape[1]
+    groups = back_ref.shape[0]
+    members = owners // groups
+
+    def partner(i):
+        total, bit = 0, 1
+        while bit < owners:
+            total = total + ((me // bit + i // bit) % 2) * bit
+            bit *= 2
+        return total
+
     q_width = wq_ref.shape[1] // 4
     kv_width = wk_ref.shape[1] // 4
 
@@ -56,7 +67,7 @@
     @pl.loop(1, owners)
     def _(i):
         pl.semaphore_signal(
-            barrier, inc=1, device_id={"dp": (me + i) % owners}, device_id_type=MESH
+            barrier, inc=1, device_id={"dp": partner(i)}, device_id_type=MESH
         )
 
     for peer in (pair, across):
@@ -69,7 +80,7 @@
             dst_ref=arrived.at[i],
             send_sem=d_send.at[i],
             recv_sem=d_recv.at[i],
-            device_id={"dp": (me + i) % owners},
+            device_id={"dp": partner(i)},
             device_id_type=MESH,
         )
 
@@ -79,7 +90,7 @@
             dst_ref=returned.at[i],
             send_sem=r_send.at[i],
             recv_sem=r_recv.at[i],
-            device_id={"dp": (me + owners - i) % owners},
+            device_id={"dp": partner(i)},
             device_id_type=MESH,
         )
 
@@ -100,8 +111,8 @@
 
     @pl.loop(1, owners)
     def _(i):
-        outgoing[i] = picked(i)
-        dispatch_copy(i).start()
+        outgoing[owners - i] = picked(owners - i)
+        dispatch_copy(owners - i).start()
 
     arrived[0] = picked(0)
 
@@ -131,52 +142,72 @@
     own_copy.start()
     project(0)
 
-    def shrink(i):
-        terms[i] = jnp.dot(arrived[i], down_ref[...], preferred_element_type=jnp.float32)
-
-    shrink(0)
-
-    @pl.loop(1, owners)
-    def _(i):
-        dispatch_copy(i).wait()
-        shrink(i)
-
-    terms_copy = tensor_copy(terms, terms_in, 3, pair)
-    terms_copy.start()
-    terms_copy.wait()
-    sums[...] = terms[...] + terms_in[...]
-    sums_copy = tensor_copy(sums, sums_in, 4, across)
-    sums_copy.start()
-    sums_copy.wait()
+    own_copy.wait()
+    part[0] = part[0] + rs1[0]
+    terms[...] = jnp.zeros_like(terms)
+
+    def pair_copy(i):
+        return tensor_copy(terms.at[i], terms_in.at[i], 3 + i, pair)
+
+    def across_copy(i):
+        return tensor_copy(sums.at[i], sums_in.at[i], 3 + owners + i, across)
 
     def expand(i):
-        shrunk = (sums[i] + sums_in[i]).astype(jnp.bfloat16)
+        shrunk = (sums[i] + sums_in[i])[:, :rank].astype(jnp.bfloat16)
         return jnp.dot(
             shrunk, up_ref[...], preferred_element_type=jnp.float32
         ).astype(jnp.bfloat16)
 
-    @pl.loop(1, owners)
+    @pl.loop(0, owners + 2)
     def _(i):
-        delta[i] = expand(i)
-        return_copy(i).start()
-
-    returned[0] = expand(0)
-    own_copy.wait()
+        @pl.when(i < owners)
+        def _():
+            @pl.when(i > 0)
+            def _():
+                dispatch_copy(i).wait()
+
+            terms[i, :, pl.ds(0, rank)] = jnp.dot(
+                arrived[i], down_ref[...], preferred_element_type=jnp.float32
+            )
+            pair_copy(i).start()
+
+        @pl.when((i >= 1) & (i <= owners))
+        def _():
+            pair_copy(i - 1).wait()
+            sums[i - 1] = terms[i - 1] + terms_in[i - 1]
+            across_copy(i - 1).start()
+
+        @pl.when(i >= 2)
+        def _():
+            across_copy(i - 2).wait()
+
+            @pl.when(i == 2)
+            def _():
+                returned[0] = expand(0)
+
+            @pl.when(i > 2)
+            def _():
+                delta[i - 2] = expand(i - 2)
+                return_copy(i - 2).start()
+
     sum_copy.wait()
-    part[0] = part[0] + rs1[0] + rs2[...]
-
-    def combine(i):
-        part[1] = part[1] + jnp.dot(
-            back_ref[i], returned[i], preferred_element_type=jnp.float32
-        )
-
+    part[0] = part[0] + rs2[...]
     part[1] = jnp.zeros(part.shape[1:], jnp.float32)
-    combine(0)
-
-    @pl.loop(1, owners)
-    def _(i):
-        return_copy(i).wait()
-        combine(i)
+
+    @pl.loop(0, groups)
+    def _(g):
+        @pl.loop(0, members)
+        def _(j):
+            @pl.when(g * members + j > 0)
+            def _():
+                return_copy(g * members + j).wait()
+
+        if members == 1:
+            block = returned[g]
+        else:
+            block = returned[pl.ds(g * members, members)]
+            block = block.reshape(members * block.shape[1], width)
+        part[1] = part[1] + jnp.dot(back_ref[g], block, preferred_element_type=jnp.float32)
 
     out_ref[...] = (part[0] + adapter_scale * part[1]).astype(jnp.bfloat16)
 
@@ -209,20 +240,21 @@
     places = jnp.arange(request_count, dtype=jnp.int32)
     earlier = (chosen[:, None] == chosen[None, :]) & (places[None, :] < places[:, None])
     order = jnp.sum(earlier.astype(jnp.int32), axis=1)
-    offset = (chosen - lax.axis_index("dp") + owners) % owners
+    offset = chosen ^ lax.axis_index("dp")
     steps = jnp.arange(step_count, dtype=jnp.int32)
     slot = (offset * slot_rows + order)[None, :] + capacity * steps[:, None]
     slot = slot.reshape(row_count)
     numbers = jnp.arange(owners * slot_rows, dtype=jnp.int32)
     dispatch = (numbers.reshape(owners, slot_rows, 1) == slot[None, None, :]).astype(jnp.bfloat16)
-    back = (numbers.reshape(owners, 1, slot_rows) == slot[None, :, None]).astype(jnp.bfloat16)
-    down = jnp.pad(adapter_down_weight[0], ((0, 0), (0, rank_pad - 3 * rank_span)))
+    groups = 2 if slot_rows % 16 == 0 and owners * slot_rows % 256 == 0 else owners
+    back = (numbers.reshape(groups, 1, -1) == slot[None, :, None]).astype(jnp.bfloat16)
+    down = adapter_down_weight[0]
     up = jnp.concatenate(
         [
-            jnp.pad(adapter_up_query[0], ((0, rank_pad - rank_span), (0, 0))),
-            jnp.pad(adapter_up_key_value[0, 0], ((rank_span, rank_pad - 2 * rank_span), (0, 0))),
+            jnp.pad(adapter_up_query[0], ((0, 3 * rank_span - rank_span), (0, 0))),
+            jnp.pad(adapter_up_key_value[0, 0], ((rank_span, 3 * rank_span - 2 * rank_span), (0, 0))),
             jnp.pad(
-                adapter_up_key_value[0, 1], ((2 * rank_span, rank_pad - 3 * rank_span), (0, 0))
+                adapter_up_key_value[0, 1], ((2 * rank_span, 0), (0, 0))
             ),
         ],
         axis=1,
@@ -253,8 +285,8 @@
             pltpu.SemaphoreType.DMA((owners,)),
             pltpu.SemaphoreType.DMA((owners,)),
             pltpu.SemaphoreType.DMA((owners,)),
-            pltpu.SemaphoreType.DMA((5,)),
-            pltpu.SemaphoreType.DMA((5,)),
+            pltpu.SemaphoreType.DMA((3 + 2 * owners,)),
+            pltpu.SemaphoreType.DMA((3 + 2 * owners,)),
         ],
         compiler_params=pltpu.CompilerParams(
             collective_id=0, has_side_effects=True, vmem_limit_bytes=52 * 1024 * 1024

time: 67.3 us -> 62 us (0.921)
  Pallas kernels: 57.2 us -> 50.5 us
  other arithmetic: 2.84 us -> 3.64 us
    pallas_call x1, Pallas kernels: 57.2 us -> 50.5 us  [shards(): pl.pallas_call(functools.partial(project_kernel, owners), out_shape=jax.S...]
    pad x1 -> x0, local copies, waits for them, and re-layouts: 1.16 us -> none  [shards(): jnp.pad(adapter_down_weight[0], ((0, 0), (0, rank_pad - 3 * rank_span)))]
    concatenate x1, other arithmetic: 0.04 us -> 0.94 us  [shards(): jnp.concatenate([jnp.pad(adapter_up_query[0], ((0, 3 * rank_span - rank_s...]
    squeeze x1, local copies, waits for them, and re-layouts: 0.01 us -> 0.89 us  [shards(): adapter_up_key_value[0, 0]]
    unnamed x15 -> x11, local copies, waits for them, and re-layouts: 1.57 us -> 2.32 us
where the time goes in v3:
time: 62 us; the launch traced here: 61.6 us
  Pallas kernels  50.5 us (81%)
  local copies, waits for them, and re-layouts  4.12 us (7%)
  other arithmetic  3.64 us (6%)
  matrix products  3.27 us (5%)
    pallas_call x1, Pallas kernels, shards(): pl.pallas_call(functools.partial(project_kernel, owners), out_shape=jax.S...  50.5 us
    unnamed x11, local copies, waits for them, and re-layouts  2.32 us
    dot_general x1, matrix products, shards(): jnp.einsum('srkgd,trkd->srkgt', head_rows, fresh_keys, preferred_element_...  1.28 us

profile of v3, /device:TPU:0, one launch (start us, length us, event | category | flops | bytes accessed | tf_op | source)
XLA Modules:
  0.0 61.6 jit_solution(10659035325625967370)
XLA Ops:
  0.0 0.0 copy-start
  0.0 0.0 copy-start.1
  0.0 0.9 %slice_bitcast_fusion.2 = (bf16[64,128]{1,0:T(8,128)(2,1)S(1)}, bf16[64,128]{1,0:T(8,128)(2,1)S(1)}) fusion(bf16[1,2,64,128]{3,2,1,0:T(8,128)(2,1)} %param.17), kind=kLoop, calls=%fused_computation.48 | loop fusion | bytes 65536 | tf_op jit(solution)/shard_map/squeeze | solution.py:255
  0.9 0.9 %fusion.35.up_ref = bf16[192,1280]{1,0:T(8,128)(2,1)S(1)} fusion(bf16[64,128]{1,0:T(8,128)(2,1)S(1)} %get-tuple-element.8, bf16[64,128]{1,0:T(8,128)(2,1)S(1)} %get-tuple-element.7, bf16[64,1024]{1,0:T(8,128)(2,1)} %bitcast.101), kind=kLoop, calls=%fused_computation.26 | loop fusion | flops 3440640 | bytes 655360 | tf_op jit(solution)/shard_map/concatenate | solution.py:252
  1.8 0.9 %convert_reduce_fusion = s32[64]{0:T(128)S(1)} fusion(s32[64]{0:T(128)} %bitcast.104), kind=kLoop, calls=%fused_computation.43 | loop fusion | flops 20416 | bytes 512 | tf_op jit(solution)/shard_map/reduce_sum | solution.py:242
  2.7 0.7 %multiply_add_fusion.2 = s32[64]{0:T(128)S(1)} fusion(s32[64]{0:T(128)S(1)} %convert_reduce_fusion, s32[]{:T(128)S(6)} %axis_index.15, s32[64,1]{0,1:T(1,128)} %param.20), kind=kLoop, calls=%fused_computation.54 | loop fusion | flops 192 | bytes 772 | tf_op jit(solution)/shard_map/add | solution.py:245
  3.4 0.1 broadcast_add_fusion
  3.5 0.1 add.70
  3.6 0.1 compare_convert_fusion.1.disp_ref
  3.7 0.1 compare_convert_fusion.back_ref
  3.8 2.2 %copy.18 = bf16[1,2048,192]{2,1,0:T(8,128)(2,1)} copy(bf16[1,2048,192]{1,2,0:T(8,128)(2,1)} %param.15) | data formatting | bytes 1572864 | tf_op args[4]
  6.0 0.0 copy-done.1
  6.0 50.5 %shard_map.109 = bf16[128,1280]{1,0:T(8,128)(2,1)S(1)} custom-call(bf16[128,2048]{1,0:T(8,128)(2,1)S(1)} %bitcast.97, bf16[8,32,128]{2,1,0:T(8,128)(2,1)S(1)} %compare_convert_fusion.1.disp_ref, bf16[2,128,128]{2,1,0:T(8,128)(2,1)S(1)} %compare_convert_fusion.back_ref, bf16[2048,192]{1,0:T(8,128)(2,1)} %bitcast.98, bf16[192,1280]{1,0:T(8,128)(2,1)S(1)} %fusion.35.up_ref, ...), custom_call_target="tpu_custom_call" | custom-call | tf_op jit(solution)/shard_map/pallas_call | solution.py:265
  56.5 0.0 copy-start.3
  56.5 0.0 copy-start.2
  56.6 1.3 %fusion.50 = (f32[2,64,8]{2,0,1:T(2,128)S(1)}, f32[2,64,1,8,2]{3,4,0,1,2:T(2,128)S(1)}) fusion(bf16[2,64,128,1]{2,1,0,3:T(8,128)(2,1)S(1)} %bitcast.103, pred[2,2]{1,0:T(4,128)(4,1)S(1)} %iota_compare_fusion.6, bf16[2,64,8,128]{3,2,1,0:T(8,128)(2,1)S(1)} %bitcast.99), kind=kOutput, calls=%fused_computation.57 | convolution fusion | flops 529408 | bytes 307204 | tf_op jit(solution)/shard_map/srkgd,trkd->srkgt/dot_general | solution.py:313
  57.9 0.0 copy-done.3
  57.9 0.1 iota_compare_fusion.5
  58.0 0.0 copy-done.2
  58.0 1.0 %fusion.49 = (f32[2,64,8]{2,0,1:T(2,128)S(1)}, f32[2,64,1,8,96]{4,3,0,1,2:T(8,128)S(1)}) fusion(bf16[64,96,128]{2,1,0:T(8,128)(2,1)S(1)} %copy-done.2, pred[64,96]{1,0:T(8,128)(4,1)S(1)} %iota_compare_fusion.5, bf16[2,64,8,128]{3,2,1,0:T(8,128)(2,1)S(1)} %bitcast.100), kind=kOutput, calls=%fused_computation.56 | convolution fusion | flops 25459712 | bytes 2238464 | tf_op jit(solution)/shard_map/srkgd,rckd->srkgc/dot_general | solution.py:309
  59.1 0.3 fusion.41
  59.4 0.4 fusion.36
  59.8 0.3 fusion.42
  60.2 0.0 copy-done
  60.2 0.6 fusion.25
  60.8 0.1 convert_element_type.41
  60.9 0.8 %copy.23 = bf16[2,64,1024]{2,1,0:T(8,128)(2,1)} copy(bf16[2,64,1024]{2,0,1:T(2,128)(2,1)S(1)} %convert_element_type.41) | data formatting | bytes 524288 | tf_op jit(solution)/shard_map/convert_element_type | solution.py:335
  (9 shorter events, 0.2 us)
Async XLA Ops:
  0.0 60.2 %copy-start = (bf16[64,96,128]{2,1,0:T(8,128)(2,1)S(1)}, bf16[64,96,128]{2,1,0:T(8,128)(2,1)}, u32[]{:S(2)}) copy-start(bf16[64,96,128]{2,1,0:T(8,128)(2,1)} %param.19) | copy-start | bytes 4718596
  0.0 6.0 %copy-start.1 = (bf16[2,64,2048]{2,1,0:T(8,128)(2,1)S(1)}, bf16[2,64,2048]{2,1,0:T(8,128)(2,1)}, u32[]{:S(2)}) copy-start(bf16[2,64,2048]{2,1,0:T(8,128)(2,1)} %param.11) | copy-start | bytes 1572868
  56.5 1.4 %copy-start.3 = (s32[64]{0:T(128)S(1)}, s32[64]{0:T(128)}, u32[]{:S(2)}) copy-start(s32[64]{0:T(128)} %param.21) | copy-start | bytes 772
  56.5 1.5 %copy-start.2 = (bf16[64,96,128]{2,1,0:T(8,128)(2,1)S(1)}, bf16[64,96,128]{2,1,0:T(8,128)(2,1)}, u32[]{:S(2)}) copy-start(bf16[64,96,128]{2,1,0:T(8,128)(2,1)} %param.18) | copy-start | bytes 4718596

commit v4 on v3

--- a/solution.py
+++ b/solution.py
@@ -15,9 +15,9 @@
 
 def project_kernel(
     owners,
-    hid_ref, disp_ref, back_ref, down_ref, up_ref, wq_ref, wk_ref, wv_ref,
+    hid_ref, disp_ref, back_ref, down_ref, up_q_ref, up_kv_ref, wq_ref, wk_ref, wv_ref,
     out_ref,
-    wbuf, part, rs1, rs2, outgoing, arrived, terms, terms_in, sums, sums_in, delta, returned,
+    wbuf, part, rs1, rs2, outgoing, arrived, terms, terms_in, sums, sums_in, delta, returned, up_ref,
     w_sem, d_send, d_recv, r_send, r_recv, x_send, x_recv,
 ):
     me = lax.axis_index("dp")
@@ -27,7 +27,8 @@
     targets = {0: t, 1: pair, 2: across, 3: (pair + 2) % 4}
     order = (3, 2, 1, 0)
     width = part.shape[2]
-    rank = down_ref.shape[1]
+    rank = down_ref.shape[0]
+    span = up_q_ref.shape[0]
     groups = back_ref.shape[0]
     members = owners // groups
 
@@ -40,6 +41,9 @@
 
     q_width = wq_ref.shape[1] // 4
     kv_width = wk_ref.shape[1] // 4
+
+    def turn(j):
+        return (j + owners // 2 - 2) % (owners - 1) + 1
 
     def weight_copies(k):
         q_cols = pl.ds(pl.multiple_of(targets[k] * q_width, 128), q_width)
@@ -110,9 +114,10 @@
         ).astype(jnp.bfloat16)
 
     @pl.loop(1, owners)
-    def _(i):
-        outgoing[owners - i] = picked(owners - i)
-        dispatch_copy(owners - i).start()
+    def _(j):
+        i = turn(j)
+        outgoing[i] = picked(i)
+        dispatch_copy(i).start()
 
     arrived[0] = picked(0)
 
@@ -145,6 +150,10 @@
     own_copy.wait()
     part[0] = part[0] + rs1[0]
     terms[...] = jnp.zeros_like(terms)
+    up_ref[...] = jnp.zeros_like(up_ref)
+    up_ref[pl.ds(0, span), pl.ds(0, q_width)] = up_q_ref[...]
+    up_ref[pl.ds(span, span), pl.ds(q_width, kv_width)] = up_kv_ref[0]
+    up_ref[pl.ds(2 * span, span), pl.ds(q_width + kv_width, kv_width)] = up_kv_ref[1]
 
     def pair_copy(i):
         return tensor_copy(terms.at[i], terms_in.at[i], 3 + i, pair)
@@ -158,44 +167,51 @@
             shrunk, up_ref[...], preferred_element_type=jnp.float32
         ).astype(jnp.bfloat16)
 
-    @pl.loop(0, owners + 2)
-    def _(i):
-        @pl.when(i < owners)
+    def shrink(i):
+        terms[i, :, pl.ds(0, rank)] = lax.dot_general(
+            arrived[i],
+            down_ref[...],
+            (((1,), (1,)), ((), ())),
+            preferred_element_type=jnp.float32,
+        )
+        pair_copy(i).start()
+
+    def reduce_pair(i):
+        pair_copy(i).wait()
+        sums[i] = terms[i] + terms_in[i]
+        across_copy(i).start()
+
+    shrink(0)
+    reduce_pair(0)
+    across_copy(0).wait()
+    returned[0] = expand(0)
+
+    @pl.loop(1, owners + 2)
+    def _(j):
+        @pl.when(j < owners)
         def _():
-            @pl.when(i > 0)
-            def _():
-                dispatch_copy(i).wait()
-
-            terms[i, :, pl.ds(0, rank)] = jnp.dot(
-                arrived[i], down_ref[...], preferred_element_type=jnp.float32
-            )
-            pair_copy(i).start()
-
-        @pl.when((i >= 1) & (i <= owners))
+            dispatch_copy(turn(j)).wait()
+            shrink(turn(j))
+
+        @pl.when((j >= 2) & (j <= owners))
         def _():
-            pair_copy(i - 1).wait()
-            sums[i - 1] = terms[i - 1] + terms_in[i - 1]
-            across_copy(i - 1).start()
-
-        @pl.when(i >= 2)
+            reduce_pair(turn(j - 1))
+
+        @pl.when(j >= 3)
         def _():
-            across_copy(i - 2).wait()
-
-            @pl.when(i == 2)
-            def _():
-                returned[0] = expand(0)
-
-            @pl.when(i > 2)
-            def _():
-                delta[i - 2] = expand(i - 2)
-                return_copy(i - 2).start()
+            i = turn(j - 2)
+            across_copy(i).wait()
+            delta[i] = expand(i)
+            return_copy(i).start()
 
     sum_copy.wait()
     part[0] = part[0] + rs2[...]
     part[1] = jnp.zeros(part.shape[1:], jnp.float32)
 
     @pl.loop(0, groups)
-    def _(g):
+    def _(count):
+        g = groups - 1 - count
+
         @pl.loop(0, members)
         def _(j):
             @pl.when(g * members + j > 0)
@@ -248,24 +264,14 @@
     dispatch = (numbers.reshape(owners, slot_rows, 1) == slot[None, None, :]).astype(jnp.bfloat16)
     groups = 2 if slot_rows % 16 == 0 and owners * slot_rows % 256 == 0 else owners
     back = (numbers.reshape(groups, 1, -1) == slot[None, :, None]).astype(jnp.bfloat16)
-    down = adapter_down_weight[0]
-    up = jnp.concatenate(
-        [
-            jnp.pad(adapter_up_query[0], ((0, 3 * rank_span - rank_span), (0, 0))),
-            jnp.pad(adapter_up_key_value[0, 0], ((rank_span, 3 * rank_span - 2 * rank_span), (0, 0))),
-            jnp.pad(
-                adapter_up_key_value[0, 1], ((2 * rank_span, 0), (0, 0))
-            ),
-        ],
-        axis=1,
-    )
+    down = adapter_down_weight[0].T
     f32, bf16 = jnp.float32, jnp.bfloat16
     vmem = pl.BlockSpec(memory_space=pltpu.VMEM)
     hbm = pl.BlockSpec(memory_space=pl.ANY)
     rows = pl.pallas_call(
         functools.partial(project_kernel, owners),
         out_shape=jax.ShapeDtypeStruct((row_count, width), bf16),
-        in_specs=[vmem] * 5 + [hbm] * 3,
+        in_specs=[vmem] * 6 + [hbm] * 3,
         out_specs=vmem,
         scratch_shapes=[
             pltpu.VMEM((4, part_width, width), bf16),
@@ -280,6 +286,7 @@
             pltpu.VMEM((owners, slot_rows, rank_pad), f32),
             pltpu.VMEM((owners, slot_rows, width), bf16),
             pltpu.VMEM((owners, slot_rows, width), bf16),
+            pltpu.VMEM((3 * rank_span, width), bf16),
             pltpu.SemaphoreType.DMA((4, 3)),
             pltpu.SemaphoreType.DMA((owners,)),
             pltpu.SemaphoreType.DMA((owners,)),
@@ -291,7 +298,7 @@
         compiler_params=pltpu.CompilerParams(
             collective_id=0, has_side_effects=True, vmem_limit_bytes=52 * 1024 * 1024
         ),
-    )(flat_rows, dispatch, back, down, up, query_weight, key_weight, value_weight)
+    )(flat_rows, dispatch, back, down, adapter_up_query[0], adapter_up_key_value[0], query_weight, key_weight, value_weight)
     query_rows = rows[:, :query_width]
     appended_keys = rows[:, query_width : query_width + kv_width]
     appended_values = rows[:, query_width + kv_width :]

time: 62 us -> 60.9 us (0.982)
  Pallas kernels: 50.5 us -> 48.9 us
  local copies, waits for them, and re-layouts: 4.12 us -> 4.84 us
    unnamed x11 -> x14, local copies, waits for them, and re-layouts: 2.32 us -> 3.92 us
    pallas_call x1, Pallas kernels: 50.5 us -> 48.9 us  [shards(): pl.pallas_call(functools.partial(project_kernel, owners), out_shape=jax.S...]
    concatenate x1 -> x0, other arithmetic: 0.94 us -> none  [shards(): jnp.concatenate([jnp.pad(adapter_up_query[0], ((0, 3 * rank_span - rank_s...]
    squeeze x1 -> x0, local copies, waits for them, and re-layouts: 0.89 us -> none  [shards(): adapter_up_key_value[0, 0]]
    lt x1, other arithmetic: 0.07 us -> 0.73 us  [shards(): jnp.arange(cache_depth, dtype=jnp.int32)[None, :] < cache_length[:, None]]
where the time goes in v4:
time: 60.9 us; the launch traced here: 60.6 us
  Pallas kernels  48.9 us (80%)
  local copies, waits for them, and re-layouts  4.84 us (8%)
  other arithmetic  3.42 us (6%)
  matrix products  3.27 us (5%)
    pallas_call x1, Pallas kernels, shards(): pl.pallas_call(functools.partial(project_kernel, owners), out_shape=jax.S...  48.9 us
    unnamed x14, local copies, waits for them, and re-layouts  3.92 us
    dot_general x1, matrix products, shards(): jnp.einsum('srkgd,trkd->srkgt', head_rows, fresh_keys, preferred_element_...  1.28 us

profile of v4, /device:TPU:0, one launch (start us, length us, event | category | flops | bytes accessed | tf_op | source)
XLA Modules:
  0.0 60.6 jit_solution(566373906071957113)
XLA Ops:
  0.0 0.0 copy-start
  0.0 1.0 %convert_reduce_fusion = s32[64]{0:T(128)S(1)} fusion(s32[64]{0:T(128)} %bitcast.104), kind=kLoop, calls=%fused_computation.33 | loop fusion | flops 20416 | bytes 512 | tf_op jit(solution)/shard_map/reduce_sum | solution.py:258
  1.0 0.7 %multiply_add_fusion.2 = s32[64]{0:T(128)S(1)} fusion(s32[64]{0:T(128)S(1)} %convert_reduce_fusion, s32[]{:T(128)S(6)} %axis_index.15, s32[64,1]{0,1:T(1,128)} %param.20), kind=kLoop, calls=%fused_computation.42 | loop fusion | flops 192 | bytes 772 | tf_op jit(solution)/shard_map/add | solution.py:261
  1.6 0.1 broadcast_add_fusion
  1.7 0.1 add.64
  1.8 0.7 %iota_compare_fusion.1 = pred[64,96]{1,0:T(8,128)(4,1)S(1)} fusion(s32[64]{0:T(128)} %param.21), kind=kLoop, calls=%fused_computation.35 | loop fusion | flops 6144 | bytes 6400 | tf_op jit(solution)/shard_map/lt | solution.py:323
  2.6 0.1 compare_convert_fusion.1.disp_ref
  2.7 0.1 compare_convert_fusion.back_ref
  2.8 0.0 copy-start.1
  2.8 1.1 %copy-done.1 = bf16[1,2048,192]{1,2,0:T(8,128)(2,1)S(1)} copy-done((bf16[1,2048,192]{1,2,0:T(8,128)(2,1)S(1)}, bf16[1,2048,192]{1,2,0:T(8,128)(2,1)}, u32[]{:S(2)}) %copy-start.1) | copy-done | bytes 786456
  3.9 0.0 copy-start.2
  3.9 1.0 %copy-done.2 = bf16[2,64,2048]{2,1,0:T(8,128)(2,1)S(1)} copy-done((bf16[2,64,2048]{2,1,0:T(8,128)(2,1)S(1)}, bf16[2,64,2048]{2,1,0:T(8,128)(2,1)}, u32[]{:S(2)}) %copy-start.2) | copy-done | bytes 524312
  4.9 0.0 copy-start.3
  4.9 0.9 %copy-done.3 = bf16[1,64,1024]{2,1,0:T(8,128)(2,1)S(1)} copy-done((bf16[1,64,1024]{2,1,0:T(8,128)(2,1)S(1)}, bf16[1,64,1024]{2,1,0:T(8,128)(2,1)}, u32[]{:S(2)}) %copy-start.3) | copy-done | bytes 131096
  5.8 0.0 copy-start.4
  5.8 0.8 %copy-done.4 = bf16[1,2,64,128]{3,2,1,0:T(8,128)(2,1)S(1)} copy-done((bf16[1,2,64,128]{3,2,1,0:T(8,128)(2,1)S(1)}, bf16[1,2,64,128]{3,2,1,0:T(8,128)(2,1)}, u32[]{:S(2)}) %copy-start.4) | copy-done | bytes 32792
  6.6 48.9 %shard_map.109 = bf16[128,1280]{1,0:T(8,128)(2,1)S(1)} custom-call(bf16[128,2048]{1,0:T(8,128)(2,1)S(1)} %bitcast.97, bf16[8,32,128]{2,1,0:T(8,128)(2,1)S(1)} %compare_convert_fusion.1.disp_ref, bf16[2,128,128]{2,1,0:T(8,128)(2,1)S(1)} %compare_convert_fusion.back_ref, bf16[192,2048]{1,0:T(8,128)(2,1)S(1)} %bitcast.96, bf16[64,1024]{1,0:T(8,128)(2,1)S(1)} %bitcast.98, ...), custom_call_target="tpu_custom_call" | custom-call | tf_op jit(solution)/shard_map/pallas_call | solution.py:271
  55.5 0.0 copy-start.5
  55.7 1.3 %fusion.44 = (f32[2,64,8]{2,0,1:T(2,128)S(1)}, f32[2,64,1,8,2]{3,4,0,1,2:T(2,128)S(1)}) fusion(bf16[2,64,128,1]{2,1,0,3:T(8,128)(2,1)S(1)} %bitcast.103, pred[2,2]{1,0:T(4,128)(4,1)S(1)} %iota_compare_fusion.2, bf16[2,64,8,128]{3,2,1,0:T(8,128)(2,1)S(1)} %bitcast.100), kind=kOutput, calls=%fused_computation.45 | convolution fusion | flops 529408 | bytes 307204 | tf_op jit(solution)/shard_map/srkgd,trkd->srkgt/dot_general | solution.py:320
  56.9 0.0 copy-done.5
  57.0 1.0 %fusion.43 = (f32[2,64,8]{2,0,1:T(2,128)S(1)}, f32[2,64,1,8,96]{4,3,0,1,2:T(8,128)S(1)}) fusion(bf16[64,96,128]{2,1,0:T(8,128)(2,1)S(1)} %copy-done.5, pred[64,96]{1,0:T(8,128)(4,1)S(1)} %iota_compare_fusion.1, bf16[2,64,8,128]{3,2,1,0:T(8,128)(2,1)S(1)} %bitcast.101), kind=kOutput, calls=%fused_computation.44 | convolution fusion | flops 25459712 | bytes 2238464 | tf_op jit(solution)/shard_map/srkgd,rckd->srkgc/dot_general | solution.py:316
  58.0 0.3 fusion.35
  58.3 0.4 fusion.30
  58.8 0.3 fusion.36
  59.1 0.0 copy-done
  59.1 0.6 %fusion.25 = bf16[2,64,1,8,128]{4,3,0,1,2:T(8,128)(2,1)S(1)} fusion(f32[64,128,2,8]{1,3,2,0:T(8,128)S(1)} %fusion.36, bf16[64,96,128]{2,1,0:T(8,128)(2,1)S(1)} %copy-done, f32[2,64,1,8,96]{4,3,0,1,2:T(8,128)S(1)} %get-tuple-element.8, f32[2,64,8]{2,0,1:T(2,128)S(1)} %add.65, f32[2,64,8]{2,0,1:T(2,128)S(1)} %max.9), kind=kOutput, calls=%fused_computation.11 | convolution fusion | flops 25722880 | bytes 2760704 | tf_op jit(solution)/shard_map/srkgc,rckd->srkgd/dot_general | solution.py:336
  59.7 0.1 convert_element_type.35
  59.8 0.8 %copy.21 = bf16[2,64,1024]{2,1,0:T(8,128)(2,1)} copy(bf16[2,64,1024]{2,0,1:T(2,128)(2,1)S(1)} %convert_element_type.35) | data formatting | bytes 524288 | tf_op jit(solution)/shard_map/convert_element_type | solution.py:342
  (9 shorter events, 0.2 us)
Async XLA Ops:
  0.0 59.1 %copy-start = (bf16[64,96,128]{2,1,0:T(8,128)(2,1)S(1)}, bf16[64,96,128]{2,1,0:T(8,128)(2,1)}, u32[]{:S(2)}) copy-start(bf16[64,96,128]{2,1,0:T(8,128)(2,1)} %param.19) | copy-start | bytes 4718596
  2.8 1.1 %copy-start.1 = (bf16[1,2048,192]{1,2,0:T(8,128)(2,1)S(1)}, bf16[1,2048,192]{1,2,0:T(8,128)(2,1)}, u32[]{:S(2)}) copy-start(bf16[1,2048,192]{1,2,0:T(8,128)(2,1)} %param.15) | copy-start | bytes 2359300
  3.9 1.0 %copy-start.2 = (bf16[2,64,2048]{2,1,0:T(8,128)(2,1)S(1)}, bf16[2,64,2048]{2,1,0:T(8,128)(2,1)}, u32[]{:S(2)}) copy-start(bf16[2,64,2048]{2,1,0:T(8,128)(2,1)} %param.11) | copy-start | bytes 1572868
  4.9 0.9 %copy-start.3 = (bf16[1,64,1024]{2,1,0:T(8,128)(2,1)S(1)}, bf16[1,64,1024]{2,1,0:T(8,128)(2,1)}, u32[]{:S(2)}) copy-start(bf16[1,64,1024]{2,1,0:T(8,128)(2,1)} %param.16) | copy-start | bytes 393220
  5.8 0.8 %copy-start.4 = (bf16[1,2,64,128]{3,2,1,0:T(8,128)(2,1)S(1)}, bf16[1,2,64,128]{3,2,1,0:T(8,128)(2,1)}, u32[]{:S(2)}) copy-start(bf16[1,2,64,128]{3,2,1,0:T(8,128)(2,1)} %param.17) | copy-start | bytes 98308
  55.5 1.4 %copy-start.5 = (bf16[64,96,128]{2,1,0:T(8,128)(2,1)S(1)}, bf16[64,96,128]{2,1,0:T(8,128)(2,1)}, u32[]{:S(2)}) copy-start(bf16[64,96,128]{2,1,0:T(8,128)(2,1)} %param.18) | copy-start | bytes 4718596

commit v5 on v4

--- a/solution.py
+++ b/solution.py
@@ -15,9 +15,10 @@
 
 def project_kernel(
     owners,
-    hid_ref, disp_ref, back_ref, down_ref, up_q_ref, up_kv_ref, wq_ref, wk_ref, wv_ref,
+    hid_hbm, disp_ref, back_ref, down_hbm, up_q_hbm, up_kv_hbm, wq_ref, wk_ref, wv_ref,
     out_ref,
     wbuf, part, rs1, rs2, outgoing, arrived, terms, terms_in, sums, sums_in, delta, returned, up_ref,
+    hid_ref, down_ref, up_q_ref, up_kv_ref, l_sem,
     w_sem, d_send, d_recv, r_send, r_recv, x_send, x_recv,
 ):
     me = lax.axis_index("dp")
@@ -62,9 +63,18 @@
             ),
         )
 
+    local_copies = [
+        pltpu.make_async_copy(hid_hbm, hid_ref, l_sem.at[0]),
+        pltpu.make_async_copy(down_hbm, down_ref, l_sem.at[1]),
+        pltpu.make_async_copy(up_q_hbm, up_q_ref, l_sem.at[2]),
+        pltpu.make_async_copy(up_kv_hbm, up_kv_ref, l_sem.at[3]),
+    ]
+    local_copies[0].start()
     for k in order:
         for copy in weight_copies(k):
             copy.start()
+    for copy in local_copies[1:]:
+        copy.start()
 
     barrier = pltpu.get_barrier_semaphore()
 
@@ -76,6 +86,7 @@
 
     for peer in (pair, across):
         pl.semaphore_signal(barrier, inc=1, device_id={"tensor": peer}, device_id_type=MESH)
+    local_copies[0].wait()
     pl.semaphore_wait(barrier, owners + 1)
 
     def dispatch_copy(i):
@@ -151,6 +162,8 @@
     part[0] = part[0] + rs1[0]
     terms[...] = jnp.zeros_like(terms)
     up_ref[...] = jnp.zeros_like(up_ref)
+    for copy in local_copies[1:]:
+        copy.wait()
     up_ref[pl.ds(0, span), pl.ds(0, q_width)] = up_q_ref[...]
     up_ref[pl.ds(span, span), pl.ds(q_width, kv_width)] = up_kv_ref[0]
     up_ref[pl.ds(2 * span, span), pl.ds(q_width + kv_width, kv_width)] = up_kv_ref[1]
@@ -267,11 +280,11 @@
     down = adapter_down_weight[0].T
     f32, bf16 = jnp.float32, jnp.bfloat16
     vmem = pl.BlockSpec(memory_space=pltpu.VMEM)
-    hbm = pl.BlockSpec(memory_space=pl.ANY)
+    hbm = pl.BlockSpec(memory_space=pltpu.HBM)
     rows = pl.pallas_call(
         functools.partial(project_kernel, owners),
         out_shape=jax.ShapeDtypeStruct((row_count, width), bf16),
-        in_specs=[vmem] * 6 + [hbm] * 3,
+        in_specs=[hbm] + [vmem] * 2 + [hbm] * 6,
         out_specs=vmem,
         scratch_shapes=[
             pltpu.VMEM((4, part_width, width), bf16),
@@ -287,6 +300,11 @@
             pltpu.VMEM((owners, slot_rows, width), bf16),
             pltpu.VMEM((owners, slot_rows, width), bf16),
             pltpu.VMEM((3 * rank_span, width), bf16),
+            pltpu.VMEM((row_count, part_width), bf16),
+            pltpu.VMEM((3 * rank_span, part_width), bf16),
+            pltpu.VMEM((rank_span, query_width), bf16),
+            pltpu.VMEM((2, rank_span, kv_width), bf16),
+            pltpu.SemaphoreType.DMA((4,)),
             pltpu.SemaphoreType.DMA((4, 3)),
             pltpu.SemaphoreType.DMA((owners,)),
             pltpu.SemaphoreType.DMA((owners,)),
@@ -296,7 +314,7 @@
             pltpu.SemaphoreType.DMA((3 + 2 * owners,)),
         ],
         compiler_params=pltpu.CompilerParams(
-            collective_id=0, has_side_effects=True, vmem_limit_bytes=52 * 1024 * 1024
+            collective_id=0, has_side_effects=True, vmem_limit_bytes=63 * 1024 * 1024
         ),
     )(flat_rows, dispatch, back, down, adapter_up_query[0], adapter_up_key_value[0], query_weight, key_weight, value_weight)
     query_rows = rows[:, :query_width]

time: 60.9 us -> 66.1 us (1.085)
  Pallas kernels: 48.9 us -> 54.5 us
  local copies, waits for them, and re-layouts: 4.84 us -> 3.4 us
  other arithmetic: 3.42 us -> 4.62 us
    pallas_call x1, Pallas kernels: 48.9 us -> 54.5 us  [shards(): pl.pallas_call(functools.partial(project_kernel, owners), out_shape=jax.S...]
    unnamed x14 -> x6, local copies, waits for them, and re-layouts: 3.92 us -> 1.59 us
    slice x1, local copies, waits for them, and re-layouts: 0.01 us -> 0.9 us  [shards(): appended_values = rows[:, query_width + kv_width:]]
where the time goes in v5:
time: 66.1 us; the launch traced here: 65.9 us
  Pallas kernels  54.5 us (82%)
  other arithmetic  4.62 us (7%)
  local copies, waits for them, and re-layouts  3.4 us (5%)
  matrix products  3.28 us (5%)
    pallas_call x1, Pallas kernels, shards(): pl.pallas_call(functools.partial(project_kernel, owners), out_shape=jax.S...  54.5 us
    unnamed x6, local copies, waits for them, and re-layouts  1.59 us

profile of v5, /device:TPU:0, one launch (start us, length us, event | category | flops | bytes accessed | tf_op | source)
XLA Modules:
  0.0 65.9 jit_solution(17440557715936808657)
XLA Ops:
  0.0 0.9 %convert_reduce_fusion = s32[64]{0:T(128)S(1)} fusion(s32[64]{0:T(128)} %bitcast.104), kind=kLoop, calls=%fused_computation.33 | loop fusion | flops 20416 | bytes 512 | tf_op jit(solution)/shard_map/reduce_sum | solution.py:271
  0.9 0.7 %multiply_add_fusion.2 = s32[64]{0:T(128)S(1)} fusion(s32[64]{0:T(128)S(1)} %convert_reduce_fusion, s32[]{:T(128)S(6)} %axis_index.15, s32[64,1]{0,1:T(1,128)} %param.20), kind=kLoop, calls=%fused_computation.42 | loop fusion | flops 192 | bytes 772 | tf_op jit(solution)/shard_map/add | solution.py:274
  1.6 0.1 broadcast_add_fusion
  1.7 0.1 add.64
  1.8 0.7 %iota_compare_fusion.1 = pred[64,96]{1,0:T(8,128)(4,1)S(1)} fusion(s32[64]{0:T(128)} %param.21), kind=kLoop, calls=%fused_computation.35 | loop fusion | flops 6144 | bytes 6400 | tf_op jit(solution)/shard_map/lt | solution.py:341
  2.5 0.7 %compare_convert_fusion.1.disp_ref = bf16[8,32,128]{2,1,0:T(8,128)(2,1)} fusion(s32[128]{0:T(128)S(1)} %add.64, s32[8,32]{1,0:T(8,128)S(1)} %multiply_add_fusion), kind=kLoop, calls=%fused_computation.26 | loop fusion | flops 65536 | bytes 67072 | tf_op jit(solution)/shard_map/convert_element_type | solution.py:277
  3.2 0.7 %compare_convert_fusion.back_ref = bf16[2,128,128]{2,1,0:T(8,128)(2,1)} fusion(s32[2,128]{1,0:T(2,128)S(1)} %multiply_add_fusion.1, s32[128]{0:T(128)S(1)} %add.64), kind=kLoop, calls=%fused_computation.25 | loop fusion | flops 65536 | bytes 67072 | tf_op jit(solution)/shard_map/convert_element_type | solution.py:279
  3.9 54.5 %shard_map.109 = bf16[128,1280]{1,0:T(8,128)(2,1)} custom-call(bf16[128,2048]{1,0:T(8,128)(2,1)} %bitcast.99, bf16[8,32,128]{2,1,0:T(8,128)(2,1)} %compare_convert_fusion.1.disp_ref, bf16[2,128,128]{2,1,0:T(8,128)(2,1)} %compare_convert_fusion.back_ref, bf16[192,2048]{1,0:T(8,128)(2,1)} %bitcast.98, bf16[64,1024]{1,0:T(8,128)(2,1)} %bitcast.100, ...), custom_call_target="tpu_custom_call" | custom-call | tf_op jit(solution)/shard_map/pallas_call | solution.py:284
  58.4 0.0 copy-start
  58.5 0.9 %fusion.42 = (bf16[128,128]{1,0:T(8,128)(2,1)S(1)}, bf16[128,128]{1,0:T(8,128)(2,1)S(1)}) fusion(bf16[128,1280]{1,0:T(8,128)(2,1)} %shard_map.109), kind=kLoop, calls=%fused_computation.43 | loop fusion | bytes 131072 | tf_op jit(solution)/shard_map/slice | solution.py:322
  59.4 1.0 %slice_bitcast_fusion = bf16[16,8,8,128]{3,1,2,0:T(8,128)(2,1)S(1)} fusion(bf16[128,1280]{1,0:T(8,128)(2,1)} %shard_map.109), kind=kLoop, calls=%fused_computation.20 | loop fusion | bytes 524288
  60.4 1.3 %fusion.44 = (f32[2,64,8]{2,0,1:T(2,128)S(1)}, f32[2,64,1,8,2]{3,4,0,1,2:T(2,128)S(1)}) fusion(bf16[2,64,128,1]{2,1,0,3:T(8,128)(2,1)S(1)} %bitcast.103, pred[2,2]{1,0:T(4,128)(4,1)S(1)} %iota_compare_fusion.2, bf16[2,64,8,128]{3,2,1,0:T(8,128)(2,1)S(1)} %bitcast.96), kind=kOutput, calls=%fused_computation.45 | convolution fusion | flops 529408 | bytes 307204 | tf_op jit(solution)/shard_map/srkgd,trkd->srkgt/dot_general | solution.py:338
  61.7 0.0 copy-done
  61.7 1.0 %fusion.43 = (f32[2,64,8]{2,0,1:T(2,128)S(1)}, f32[2,64,1,8,96]{4,3,0,1,2:T(8,128)S(1)}) fusion(bf16[64,96,128]{2,1,0:T(8,128)(2,1)S(1)} %copy-done, pred[64,96]{1,0:T(8,128)(4,1)S(1)} %iota_compare_fusion.1, bf16[2,64,8,128]{3,2,1,0:T(8,128)(2,1)S(1)} %bitcast.97), kind=kOutput, calls=%fused_computation.44 | convolution fusion | flops 25459712 | bytes 2238464 | tf_op jit(solution)/shard_map/srkgd,rckd->srkgc/dot_general | solution.py:334
  62.8 0.3 fusion.35
  63.0 0.0 copy-start.1
  63.0 0.4 fusion.30
  63.5 0.3 fusion.36
  63.9 0.6 copy-done.1
  64.4 0.6 fusion.25
  65.0 0.1 convert_element_type.35
  65.1 0.8 %copy.21 = bf16[2,64,1024]{2,1,0:T(8,128)(2,1)} copy(bf16[2,64,1024]{2,0,1:T(2,128)(2,1)S(1)} %convert_element_type.35) | data formatting | bytes 524288 | tf_op jit(solution)/shard_map/convert_element_type | solution.py:360
  (7 shorter events, 0.1 us)
Async XLA Ops:
  58.4 3.2 %copy-start = (bf16[64,96,128]{2,1,0:T(8,128)(2,1)S(1)}, bf16[64,96,128]{2,1,0:T(8,128)(2,1)}, u32[]{:S(2)}) copy-start(bf16[64,96,128]{2,1,0:T(8,128)(2,1)} %param.18) | copy-start | bytes 4718596
  63.0 1.4 %copy-start.1 = (bf16[64,96,128]{2,1,0:T(8,128)(2,1)S(1)}, bf16[64,96,128]{2,1,0:T(8,128)(2,1)}, u32[]{:S(2)}) copy-start(bf16[64,96,128]{2,1,0:T(8,128)(2,1)} %param.19) | copy-start | bytes 4718596
